TPU v7x, 32 devices: a whole 2x2x4 slice. The times are simulated.
32 devices in a mesh: seq: 8 (over y, x, core), chan: 4 (over z).
Axes of the slice: x: 2, y: 2, z: 4, core: 2. Of those that a mesh axis runs over, the one named last changes fastest.
Arguments:
- tokens: int32 [2048], P('seq'), may hold values from 0 to 511
- embedding: bfloat16 [512, 4096], P(None, 'chan'), may hold values from -6 to 6
- norm_gain: float32 [4096], replicated, may hold values from 0.5 to 1.5
- in_weight: bfloat16 [4096, 3, 4096], P(None, None, 'chan'), may hold values from -0.09375 to 0.09375
- short_filter: float32 [3, 3, 4096], P(None, None, 'chan'), may hold values from -3 to 3
- decay_rate: float32 [16, 4096], P(None, 'chan'), may hold values from 9.765625e-06 to 0.025, as said below
- residue: float32 [16, 4096], P(None, 'chan'), may hold values from -0.06 to 0.06
- skip_gain: float32 [4096], P('chan'), may hold values from -4 to 4
- out_weight: bfloat16 [4096, 4096], P('chan'), may hold values from -0.125 to 0.125
Outputs:
- block_out: bfloat16 [2048, 4096], P('seq', 'chan')
Inputs may be any that keep to these rules, and one draw needn't show every extreme that they name: `decay_rate`: positive rates.
All inputs are finite; a program needn't handle non-finite values.
Results may differ from a plain program's by a relative error of at most 0.0091.
Values may be sent and summed in bfloat16 or wider, within the bound.
A program may use at most 256 MiB of HBM per device.

v0:
```python
import jax
import jax.numpy as jnp
from jax import lax
from jax.sharding import PartitionSpec as P

FEAT = 3
BLK = 128


def from_behind(value, axis, by):
    devices = lax.axis_size(axis)
    pairs = [(i, i + by) for i in range(devices) if 0 <= i + by < devices]
    return lax.ppermute(value, axis, pairs)


def carried_in(part, axis, combine, identity):
    place = lax.axis_index(axis)
    gathered = jax.tree.map(lambda a: lax.all_gather(a, axis), part)
    state = jax.tree.map(lambda a, e: jnp.zeros_like(a) + jnp.asarray(e, a.dtype), part, identity)

    def one(lap, state):
        return combine(
            state, jax.tree.map(lambda a: lax.dynamic_index_in_dim(a, lap, 0, False), gathered)
        )

    return lax.fori_loop(0, place, one, state)


def combine(earlier, later):
    return (earlier[0] * later[0], later[0] * earlier[1] + later[1])


def on_device(
    tokens,
    embedding,
    norm_gain,
    in_weight,
    short_filter,
    decay_rate,
    residue,
    skip_gain,
    out_weight,
):
    token_rows = tokens.shape[0]
    vocab_size = embedding.shape[0]
    channels = embedding.shape[1]
    one_hot = (tokens[:, None] == jnp.arange(vocab_size, dtype=jnp.int32)[None, :]).astype(
        jnp.bfloat16
    )
    stream = jnp.dot(one_hot, embedding, preferred_element_type=jnp.float32).astype(jnp.bfloat16)
    gathered = lax.all_gather(stream, "chan", axis=1, tiled=True)
    gathered_f = gathered.astype(jnp.float32)
    scale = lax.rsqrt(jnp.mean(gathered_f * gathered_f, axis=1, keepdims=True) + 1e-06)
    normed = (gathered_f * scale * norm_gain[None, :]).astype(jnp.bfloat16)
    proj = jnp.einsum("td,djc->tjc", normed, in_weight, preferred_element_type=jnp.float32).astype(
        jnp.bfloat16
    )
    rim_rows = FEAT - 1
    earlier_rim = from_behind(proj[token_rows - rim_rows :], "seq", 1)
    padded = jnp.concatenate([earlier_rim, proj], axis=0).astype(jnp.float32)
    feat = short_filter[0][None] * padded[rim_rows : rim_rows + token_rows]
    for offset in range(1, FEAT):
        feat = (
            feat
            + short_filter[offset][None]
            * padded[rim_rows - offset : rim_rows - offset + token_rows]
        )
    feat = feat.astype(jnp.bfloat16)
    query = feat[:, 0].astype(jnp.float32)
    driven = feat[:, 1].astype(jnp.float32) * feat[:, 2].astype(jnp.float32)
    num_blocks = token_rows // BLK
    steps_f = jnp.arange(BLK, dtype=jnp.float32)
    lag_table = jnp.arange(BLK)[:, None] - jnp.arange(BLK)[None, :]
    causal = lag_table >= 0
    impulse = jnp.sum(
        residue[:, None, :] * jnp.exp(-decay_rate[:, None, :] * steps_f[None, :, None]), axis=0
    )
    toeplitz = jnp.where(causal[:, :, None], impulse[jnp.clip(lag_table, 0, BLK - 1)], 0.0)
    w_end = jnp.exp(-decay_rate[:, None, :] * (BLK - 1 - steps_f)[None, :, None])
    r_next = residue[:, None, :] * jnp.exp(-decay_rate[:, None, :] * (steps_f + 1.0)[None, :, None])
    blocks = driven.reshape(num_blocks, BLK, channels)
    intra = jnp.einsum("ijc,bjc->bic", toeplitz, blocks, precision=lax.Precision.HIGHEST)
    block_ends = jnp.einsum("njc,bjc->bnc", w_end, blocks, precision=lax.Precision.HIGHEST)
    block_ids = jnp.arange(num_blocks)
    block_gap = block_ids[:, None] - 1 - block_ids[None, :]
    gap_weight = jnp.exp(
        -decay_rate[None, None]
        * (BLK * jnp.maximum(block_gap, 0)).astype(jnp.float32)[:, :, None, None]
    )
    gap_weight = jnp.where((block_gap >= 0)[:, :, None, None], gap_weight, 0.0)
    inner_state = jnp.einsum(
        "xync,ync->xnc", gap_weight, block_ends, precision=lax.Precision.HIGHEST
    )
    tail_weight = jnp.exp(
        -decay_rate[None] * (BLK * (num_blocks - 1 - block_ids)).astype(jnp.float32)[:, None, None]
    )
    device_end = jnp.sum(tail_weight * block_ends, axis=0)
    decay_span = jnp.exp(-decay_rate * token_rows)
    identity = (jnp.ones_like(decay_span), jnp.zeros_like(device_end))
    _, incoming = carried_in((decay_span, device_end), "seq", combine, identity)
    start_weight = jnp.exp(-decay_rate[None] * (BLK * block_ids).astype(jnp.float32)[:, None, None])
    block_in = inner_state + start_weight * incoming[None]
    carried = jnp.einsum("njc,bnc->bjc", r_next, block_in, precision=lax.Precision.HIGHEST)
    long_out = (intra + carried).reshape(token_rows, channels) + skip_gain[None, :] * driven
    hidden = (query * long_out).astype(jnp.bfloat16)
    summed = lax.psum_scatter(
        lax.dot_general(
            out_weight, hidden, (((0,), (1,)), ((), ())), preferred_element_type=jnp.float32
        ),
        "chan",
        scatter_dimension=0,
        tiled=True,
    )
    mixed = summed.T
    return (stream.astype(jnp.float32) + mixed).astype(jnp.bfloat16)


def solution(mesh):
    placed = (
        P("seq"),
        P(None, "chan"),
        P(),
        P(None, None, "chan"),
        P(None, None, "chan"),
        P(None, "chan"),
        P(None, "chan"),
        P("chan"),
        P("chan", None),
    )
    return jax.shard_map(
        on_device, mesh=mesh, in_specs=placed, out_specs=P("seq", "chan"), check_vma=False
    )
```

profile of v0, /device:TPU:0, one launch (start us, length us, event | category | flops | bytes accessed | tf_op | source)
XLA Modules:
  0.0 482.6 jit_solution(14055775582244824468)
XLA Ops:
  6.5 0.0 copy-start
  6.5 0.0 all-gather.4.cloned.1.call-start
  6.5 1.2 copy-done
  7.8 2.0 convolution_convert_fusion
  9.7 0.0 all-gather.4.cloned.1.call-update
  9.7 0.0 copy-start.20
  9.8 0.0 reduce-scatter.2.cloned.1.call-start
  9.8 0.9 multiply_exponential_fusion
  10.7 0.0 copy-start.5
  10.7 0.2 copy.47
  10.9 0.0 copy-start.7
  10.9 1.1 copy.46
  12.0 0.0 copy-start.10
  12.0 0.5 iota_add_fusion
  12.5 0.5 multiply_convert_fusion.1
  13.1 0.5 iota_subtract_fusion.1
  13.6 0.6 subtract_compare_fusion
  14.2 12.3 %all-gather = f32[128,1024]{1,0:T(8,128)} all-gather(f32[16,1024]{1,0:T(8,128)S(1)} %get-tuple-element.65), channel_id=2, replica_groups=mesh['seq'=8,'chan'=4] {'seq'}, dimensions={0}, use_global_device_ids=true | all-gather | bytes 589824 | tf_op jit(solution)/shard_map/all_gather | solution.py:18
  26.6 0.6 fusion.49
  27.1 0.7 multiply_convert_fusion
  27.8 0.0 copy-done.16
  27.8 0.6 slice_bitcast_fusion.3
  28.5 11.7 %multiply_reduce_fusion = f32[128,1024]{0,1:T(8,128)S(1)} fusion(f32[16,1024]{0,1:T(8,128)S(1)} %copy.47, f32[16,1024]{0,1:T(8,128)S(1)} %copy.46), kind=kLoop, calls=%fused_computation.14 | loop fusion | flops 6160384 | bytes 655360 | tf_op jit(solution)/shard_map/reduce_sum | solution.py:75
  40.2 18.3 %all-gather.4.cloned.1.call-done = bf16[256,4096]{1,0:T(8,128)(2,1)} async-done(((bf16[256,1024]{1,0:T(8,128)(2,1)}), bf16[256,4096]{1,0:T(8,128)(2,1)}) %all-gather.4.cloned.1.call-update) | async-done | bytes 2097168 | tf_op jit(solution)/shard_map/all_gather | solution.py:51
  58.5 2.1 fusion.11
  60.6 0.0 copy-done.20
  60.6 12.5 %fusion.27 = bf16[256,3,1024]{2,0,1:T(8,128)(2,1)S(1)} fusion(bf16[4096,3,1024]{2,0,1:T(8,128)(2,1)} %param.14, bf16[256,4096]{1,0:T(8,128)(2,1)} %all-gather.4.cloned.1.call-done, f32[4096]{0:T(1024)S(1)} %copy-done.20, f32[256]{0:T(256)S(1)} %add_rsqrt_fusion), kind=kOutput, calls=%fused_computation.36 | convolution fusion | flops 6447431680 | bytes 28853248 | tf_op jit(solution)/shard_map/td,djc->tjc/dot_general | solution.py:55
  73.2 0.0 copy-done.5
  73.2 0.0 copy-done.7
  73.2 0.7 slice.42
  73.9 2.3 collective-permute-start
  76.2 0.5 multiply_convert_fusion.2
  76.7 0.2 copy.48
  76.9 70.8 %gather_fusion = f32[16384,1024]{1,0:T(8,128)} fusion(f32[128,1024]{1,0:T(8,128)S(1)} %copy.48, s32[16384]{0:T(1024)S(1)} %fusion.48), kind=kCustom, calls=%fused_computation | custom fusion | bytes 134283264 | tf_op jit(solution)/shard_map/gather | solution.py:78
  147.7 70.7 %copy.49 = f32[128,128,1024]{1,0,2:T(8,128)} copy(f32[128,128,1024]{2,1,0:T(8,128)} %bitcast.11) | data formatting | bytes 134217728 | tf_op jit(solution)/shard_map/gather | solution.py:78
  218.3 0.0 collective-permute-done
  218.3 0.0 copy-done.3
  218.3 1.2 maximum_convert_fusion
  219.6 1.0 fusion.20
  220.6 0.0 copy-start.8
  220.6 0.0 copy-start.23
  220.6 0.0 copy-start.24
  220.6 1.2 convert_multiply_fusion.3
  221.8 2.2 copy.50
  224.0 0.0 copy-done.23
  224.0 19.5 %fusion.39 = (f32[16,1024]{0,1:T(8,128)}, f32[1024,2,16]{2,1,0:T(2,128)}) fusion(f32[16,1024]{0,1:T(8,128)S(1)} %copy-done.8, f32[2]{0:T(128)S(1)} %copy-done.23, f32[2,128,1024]{1,0,2:T(2,128)} %copy.50, f32[128]{0:T(128)S(1)} %copy-done.24), kind=kOutput, calls=%fused_computation.49 | convolution fusion | flops 52510720 | bytes 1311240 | tf_op jit(solution)/shard_map/njc,bjc->bnc/dot_general | solution.py:83
  243.5 1.4 copy.64
  244.9 0.1 multiply_reduce_fusion.1
  245.1 1.3 copy.63
  246.3 1.2 copy.53
  247.5 10.3 %all-gather.1 = f32[128,1024]{1,0:T(8,128)S(1)} all-gather(f32[16,1024]{1,0:T(8,128)S(1)} %copy.53), channel_id=3, replica_groups=mesh['seq'=8,'chan'=4] {'seq'}, dimensions={0}, use_global_device_ids=true | all-gather | bytes 589824 | tf_op jit(solution)/shard_map/all_gather | solution.py:18
  257.8 0.2 copy.54
  258.1 108.9 %fusion = f32[1024,2,128]{2,1,0:T(2,128)S(1)} fusion(f32[2,128,1024]{1,0,2:T(2,128)} %copy.50, f32[128,128,1024]{1,0,2:T(8,128)} %copy.49, pred[128,128]{1,0:T(8,128)(4,1)S(1)} %copy-done.12), kind=kOutput, calls=%fused_computation.3 | convolution fusion | flops 419430400 | bytes 69222400 | tf_op jit(solution)/shard_map/ijc,bjc->bic/dot_general | solution.py:82
  367.0 0.0 copy-done.11
  367.1 0.0 copy-done.21
  367.1 0.0 copy-done.22
  367.1 0.0 copy-start.17
  367.1 14.0 %fusion.33 = f32[2,128,1024]{1,0,2:T(2,128)} fusion(f32[1024,2,128]{2,1,0:T(2,128)S(1)} %fusion, f32[128]{0:T(128)S(1)} %copy-done.21, f32[16,1024]{0,1:T(8,128)S(1)} %copy-done.9, f32[16,1024]{0,1:T(8,128)S(1)} %copy-done.11, f32[16,1024,2]{0,2,1:T(2,128)S(1)} %copy-done.4, f32[16,1024]{0,1:T(8,128)S(1)} %copy.54, f32[2]{0:T(128)S(1)} %copy-done.22), kind=kOutput, calls=%fused_computation.39 | convolution fusion | flops 54886400 | bytes 2425352 | tf_op jit(solution)/shard_map/njc,bnc->bjc/dot_general | solution.py:103
  381.1 2.3 copy.55
  383.4 1.5 fusion.36
  384.9 7.7 %convolution_bitcast_fusion = f32[4096,256]{0,1:T(8,128)} fusion(bf16[256,1024]{1,0:T(8,128)(2,1)S(1)} %fusion.36, bf16[1024,4096]{1,0:T(8,128)(2,1)} %param.19), kind=kOutput, calls=%fused_computation.15 | convolution fusion | flops 2147483648 | bytes 13107200 | tf_op jit(solution)/shard_map/dot_general | solution.py:107
  392.6 0.0 reduce-scatter.2.cloned.1.call-update
  392.6 81.0 %reduce-scatter.2.cloned.1.call-done = f32[1024,256]{0,1:T(8,128)} async-done(((f32[4096,256]{0,1:T(8,128)}), f32[1024,256]{0,1:T(8,128)}) %reduce-scatter.2.cloned.1.call-update) | async-done | bytes 1048592 | tf_op jit(solution)/shard_map/reduce_scatter | solution.py:106
  473.6 2.2 fusion.37
  (36 shorter events, 0.1 us)
Async XLA Ops:
  6.5 1.2 copy-start
  6.5 21.3 %copy-start.16 = (f32[3,3,1024]{2,1,0:T(4,128)S(1)}, f32[3,3,1024]{2,1,0:T(4,128)}, u32[]{:S(2)}) copy-start(f32[3,3,1024]{2,1,0:T(4,128)} %param.15) | copy-start | bytes 110596
  6.5 52.0 %all-gather.4.cloned.1.call-start = ((), (), s32[]{:S(2)}) async-start(), calls=%async_computation.1 | async-start | bytes 2621440 | tf_op jit(solution)/shard_map/all_gather | solution.py:51
  9.7 50.9 %copy-start.20 = (f32[4096]{0:T(1024)S(1)}, f32[4096]{0:T(1024)}, u32[]{:S(2)}) copy-start(f32[4096]{0:T(1024)} %param.13) | copy-start | bytes 49156
  9.8 463.8 %reduce-scatter.2.cloned.1.call-start = ((), (), s32[]{:S(2)}) async-start(), calls=%async_computation.2 | async-start | bytes 5242880 | tf_op jit(solution)/shard_map/reduce_scatter | solution.py:106
  10.7 62.5 %copy-start.5 = (f32[16,1024]{1,0:T(8,128)}, f32[16,1024]{1,0:T(8,128)S(1)}, u32[]{:S(2)}) copy-start(f32[16,1024]{1,0:T(8,128)S(1)} %get-tuple-element.66) | copy-start | bytes 196612
  10.9 62.3 %copy-start.7 = (f32[16,1024]{0,1:T(8,128)}, f32[16,1024]{0,1:T(8,128)S(1)}, u32[]{:S(2)}) copy-start(f32[16,1024]{0,1:T(8,128)S(1)} %copy.47) | copy-start | bytes 196612
  12.0 61.2 %copy-start.10 = (f32[16,1024]{0,1:T(8,128)}, f32[16,1024]{0,1:T(8,128)S(1)}, u32[]{:S(2)}) copy-start(f32[16,1024]{0,1:T(8,128)S(1)} %copy.46) | copy-start | bytes 196612
  73.2 3.5 copy-start.2
  73.9 144.5 %collective-permute-start = (bf16[2,3,1024]{2,0,1:T(2,128)(2,1)}, bf16[2,3,1024]{2,0,1:T(2,128)(2,1)}, u32[]{:S(2)}, u32[]{:S(2)}) collective-permute-start(bf16[2,3,1024]{2,0,1:T(2,128)(2,1)} %slice.42), channel_id=1, source_target_pairs={{0,4},{4,8},{8,12},{12,16},{16,20},{20,24},{24,28},{1,5},{5,9},{9,... | collective-permute-start | bytes 36872 | tf_op jit(solution)/shard_map/ppermute | solution.py:13
  147.7 70.7 %copy-start.3 = (bf16[256,3,1024]{2,0,1:T(8,128)(2,1)S(1)}, bf16[256,3,1024]{2,0,1:T(8,128)(2,1)}, u32[]{:S(2)}) copy-start(bf16[256,3,1024]{2,0,1:T(8,128)(2,1)} %copy-done.2) | copy-start | bytes 4718596
  218.3 1.2 copy-start.13
  218.3 1.2 copy-start.14
  218.3 1.2 copy-start.15
  220.6 3.4 copy-start.8
  220.6 3.4 copy-start.23
  220.6 3.4 copy-start.24
  224.0 20.9 %copy-start.6 = (f32[16,1024]{1,0:T(8,128)S(1)}, f32[16,1024]{1,0:T(8,128)}, u32[]{:S(2)}) copy-start(f32[16,1024]{1,0:T(8,128)} %copy-done.5) | copy-start | bytes 196612
  224.0 20.9 %copy-start.18 = (f32[2,2]{1,0:T(2,128)S(1)}, f32[2,2]{1,0:T(2,128)}, u32[]{:S(2)}) copy-start(f32[2,2]{1,0:T(2,128)} %multiply_convert_fusion) | copy-start | bytes 52
  224.0 20.9 %copy-start.19 = (pred[2,2]{1,0:T(4,128)(4,1)S(1)}, pred[2,2]{1,0:T(4,128)(4,1)}, u32[]{:S(2)}) copy-start(pred[2,2]{1,0:T(4,128)(4,1)} %fusion.49) | copy-start | bytes 16
  243.5 14.5 %copy-start.12 = (pred[128,128]{1,0:T(8,128)(4,1)S(1)}, pred[128,128]{1,0:T(8,128)(4,1)}, u32[]{:S(2)}) copy-start(pred[128,128]{1,0:T(8,128)(4,1)} %subtract_compare_fusion) | copy-start | bytes 49156
  258.0 109.0 %copy-start.4 = (f32[16,1024,2]{0,2,1:T(2,128)S(1)}, f32[16,1024,2]{0,2,1:T(2,128)}, u32[]{:S(2)}) copy-start(f32[16,1024,2]{0,2,1:T(2,128)} %copy.63) | copy-start | bytes 393220
  258.0 109.0 %copy-start.9 = (f32[16,1024]{0,1:T(8,128)S(1)}, f32[16,1024]{0,1:T(8,128)}, u32[]{:S(2)}) copy-start(f32[16,1024]{0,1:T(8,128)} %copy-done.7) | copy-start | bytes 196612
  258.0 109.0 %copy-start.11 = (f32[16,1024]{0,1:T(8,128)S(1)}, f32[16,1024]{0,1:T(8,128)}, u32[]{:S(2)}) copy-start(f32[16,1024]{0,1:T(8,128)} %copy-done.10) | copy-start | bytes 196612
  258.1 109.0 %copy-start.21 = (f32[128]{0:T(128)S(1)}, f32[128]{0:T(128)}, u32[]{:S(2)}) copy-start(f32[128]{0:T(128)} %iota_add_fusion) | copy-start | bytes 1540
  258.1 109.0 %copy-start.22 = (f32[2]{0:T(128)S(1)}, f32[2]{0:T(128)}, u32[]{:S(2)}) copy-start(f32[2]{0:T(128)} %multiply_convert_fusion.2) | copy-start | bytes 28
  367.1 16.3 %copy-start.17 = (f32[1024]{0:T(1024)S(1)}, f32[1024]{0:T(1024)}, u32[]{:S(2)}) copy-start(f32[1024]{0:T(1024)} %param.18) | copy-start | bytes 12292
  392.6 81.0 %copy-start.1 = (bf16[256,1024]{1,0:T(8,128)(2,1)S(1)}, bf16[256,1024]{1,0:T(8,128)(2,1)}, u32[]{:S(2)}) copy-start(bf16[256,1024]{1,0:T(8,128)(2,1)} %convolution_convert_fusion) | copy-start | bytes 1572868
Sparse Core Ops, SparseCore 0:
  9.9 48.6 all-gather.3
  392.7 80.8 reduce-scatter.1
where the time goes:
time: 485 us; the launch traced here: 483 us
  matrix products  165 us (34%)
  local copies, waits for them, and re-layouts  154 us (32%)
  waiting for transfers between devices  99.3 us (20%)
  other arithmetic  25.9 us (5%)
  blocking collectives  22.6 us (5%)
  between operations  13.8 us (3%)
    gather x2, local copies, waits for them, and re-layouts, on_device(): impulse[jnp.clip(lag_table, 0, BLK - 1)]  141 us
    dot_general x1, matrix products, on_device(): jnp.einsum('ijc,bjc->bic', toeplitz, blocks, precision=lax.Precision.HIGH...  109 us
    reduce_scatter x1, waiting for transfers between devices, on_device(): lax.psum_scatter(lax.dot_general(out_weight, hidden, (((0,), (1,)), ((),...  81 us
    all_gather x2, blocking collectives, carried_in(): gathered = jax.tree.map(lambda a: lax.all_gather(a, axis), part)  22.6 us
    dot_general x1, matrix products, on_device(): jnp.einsum('njc,bjc->bnc', w_end, blocks, precision=lax.Precision.HIGHEST)  19.5 us
    all_gather x1, waiting for transfers between devices, on_device(): gathered = lax.all_gather(stream, 'chan', axis=1, tiled=True)  18.3 us
    dot_general x1, matrix products, on_device(): jnp.einsum('njc,bnc->bjc', r_next, block_in, precision=lax.Precision.HIGH...  14 us
    dot_general x1, matrix products, on_device(): jnp.einsum('td,djc->tjc', normed, in_weight, preferred_element_type=jnp.f...  12.5 us
  transfers between devices with their start and end apart: 3, of which 2 were waited for; matrix products, arithmetic and copies ran while one was open for 33% of the time, Pallas kernels for 0%

commit v1 on v0

v1 whole, which is shorter than its diff:
```python
import functools

import jax
import jax.numpy as jnp
from jax import lax
from jax.experimental import pallas as pl
from jax.experimental.pallas import tpu as pltpu
from jax.sharding import PartitionSpec as P

FEAT = 3
LANES = 128
SEGS = 8
MESH = pl.DeviceIdType.MESH


def block_kernel(
    seq_size,
    chan_size,
    proj_ref,
    stream_ref,
    filter_ref,
    decay_ref,
    residue_ref,
    skip_ref,
    weight_ref,
    out_ref,
    weight_buf,
    rim_out,
    rim_in,
    padded,
    query_buf,
    driven_buf,
    seg_ends,
    own_end,
    all_ends,
    incoming,
    seg_starts,
    hidden_f,
    hidden,
    part,
    sums_out,
    sums_in,
    weight_sem,
    rim_sem,
    end_send_sem,
    end_recv_sem,
    sum_send_sem,
    sum_recv_sem,
):
    place = lax.axis_index("seq")
    shard = lax.axis_index("chan")
    rows, channels = stream_ref.shape
    modes = decay_ref.shape[0]
    groups = channels // LANES
    seg = rows // SEGS

    weight_copies = [
        pltpu.make_async_copy(
            weight_ref.at[:, pl.ds(d * channels, channels)], weight_buf.at[d], weight_sem.at[d]
        )
        for d in range(chan_size)
    ]
    for copy in weight_copies:
        copy.start()

    barrier = pltpu.get_barrier_semaphore()
    for k in range(1, seq_size):
        pl.semaphore_signal(
            barrier, 1, device_id={"seq": lax.rem(place + k, seq_size)}, device_id_type=MESH
        )
    for k in range(1, chan_size):
        pl.semaphore_signal(
            barrier, 1, device_id={"chan": lax.rem(shard + k, chan_size)}, device_id_type=MESH
        )
    for j in range(FEAT):
        rim_out[j] = proj_ref[j, rows - 16 :, :].astype(jnp.float32)[8:]
    pl.semaphore_wait(barrier, seq_size - 1 + chan_size - 1)

    rim_copy = pltpu.make_async_remote_copy(
        src_ref=rim_out,
        dst_ref=rim_in,
        send_sem=rim_sem.at[0],
        recv_sem=rim_sem.at[1],
        device_id={"seq": lax.rem(place + 1, seq_size)},
        device_id_type=MESH,
    )
    rim_copy.start()
    rim_copy.wait()
    keep = (place > 0).astype(jnp.float32)

    def spread(value):
        return jnp.broadcast_to(value[:, None, :], (value.shape[0], SEGS, LANES))

    def first_pass(g, carry):
        lanes = pl.ds(pl.multiple_of(g * LANES, LANES), LANES)
        feat = []
        for j in range(FEAT):
            now = proj_ref[j, :, lanes].astype(jnp.float32)
            padded[j, 8:, :] = now
            padded[j, :8, :] = rim_in[j, :, lanes] * keep
            total = filter_ref[j : j + 1, lanes] * now
            for offset in range(1, FEAT):
                row = offset * FEAT + j
                total = total + filter_ref[row : row + 1, lanes] * padded[j, pl.ds(8 - offset, rows), :]
            feat.append(total.astype(jnp.bfloat16).astype(jnp.float32))
        query_buf[g] = feat[0]
        driven_buf[g] = feat[1] * feat[2]
        decay = decay_ref[:, lanes]
        lam = spread(jnp.exp(-decay))

        def step(i, state):
            x = driven_buf[g, pl.ds(i, SEGS, stride=seg), :]
            return lam * state + x[None]

        state = lax.fori_loop(
            0, seg, step, jnp.zeros((modes, SEGS, LANES), jnp.float32), unroll=8
        )
        seg_ends[g] = state
        lam_seg = jnp.exp(-decay * seg)
        end = state[:, 0, :]
        for s in range(1, SEGS):
            end = lam_seg * end + state[:, s, :]
        own_end[:, lanes] = end
        return carry

    lax.fori_loop(0, groups, first_pass, 0)

    def end_copy(to, source):
        return pltpu.make_async_remote_copy(
            src_ref=own_end,
            dst_ref=all_ends.at[source],
            send_sem=end_send_sem.at[to],
            recv_sem=end_recv_sem.at[source],
            device_id={"seq": to},
            device_id_type=MESH,
        )

    for k in range(1, seq_size):
        end_copy(lax.rem(place + k, seq_size), place).start()
    for k in range(1, seq_size):
        peer = lax.rem(place + k, seq_size)
        end_copy(peer, place).wait_send()
        end_copy(peer, peer).wait_recv()
    all_ends[place] = own_end[...]

    span = jnp.exp(-decay_ref[...] * rows)
    state = jnp.zeros((modes, channels), jnp.float32)
    for p in range(seq_size - 1):
        state = jnp.where(p < place, span * state + all_ends[p], state)
    incoming[...] = state

    def second_pass(g, carry):
        lanes = pl.ds(pl.multiple_of(g * LANES, LANES), LANES)
        decay = decay_ref[:, lanes]
        lam_seg = jnp.exp(-decay * seg)
        start = incoming[:, lanes]
        for s in range(SEGS):
            seg_starts[:, s, :] = start
            start = lam_seg * start + seg_ends[g, :, s, :]
        lam = spread(jnp.exp(-decay))
        gain = spread(residue_ref[:, lanes])
        skip = jnp.broadcast_to(skip_ref[:, lanes], (SEGS, LANES))

        def step(i, state):
            at = pl.ds(i, SEGS, stride=seg)
            x = driven_buf[g, at, :]
            state = lam * state + x[None]
            long = jnp.sum(gain * state, axis=0) + skip * x
            hidden_f[at, :] = query_buf[g, at, :] * long
            return state

        lax.fori_loop(0, seg, step, seg_starts[...], unroll=8)
        hidden[:, lanes] = hidden_f[...].astype(jnp.bfloat16)
        return carry

    lax.fori_loop(0, groups, second_pass, 0)
    for copy in weight_copies:
        copy.wait()

    tile = min(256, channels)

    def project(dest):
        def one(t, carry):
            cols = pl.ds(pl.multiple_of(t * tile, tile), tile)
            part[:, cols] = jnp.dot(
                hidden[...], weight_buf[dest, :, cols], preferred_element_type=jnp.float32
            )
            return carry

        lax.fori_loop(0, channels // tile, one, 0)

    def sum_copy(way, dest, to):
        return pltpu.make_async_remote_copy(
            src_ref=sums_out.at[way, dest],
            dst_ref=sums_in.at[way, dest],
            send_sem=sum_send_sem.at[way, dest],
            recv_sem=sum_recv_sem.at[way, dest],
            device_id={"chan": to},
            device_id_type=MESH,
        )

    last = chan_size - 1

    def pass_on(way, dest, to, has_earlier):
        project(dest)

        @pl.when(has_earlier)
        def _():
            sum_copy(way, dest, to).wait_recv()
            sums_out[way, dest] = (part[...] + sums_in[way, dest].astype(jnp.float32)).astype(
                jnp.bfloat16
            )

        @pl.when(jnp.logical_not(has_earlier))
        def _():
            sums_out[way, dest] = part[...].astype(jnp.bfloat16)

        sum_copy(way, dest, to).start()

    def sum_step(t, carry):
        up = last - (t - shard)

        @pl.when((t >= shard) & (up > shard))
        def _():
            pass_on(0, up, shard + 1, shard > 0)

        down = t - (last - shard)

        @pl.when((down >= 0) & (down < shard))
        def _():
            pass_on(1, down, shard - 1, shard < last)

        return carry

    lax.fori_loop(0, 2 * last, sum_step, 0)

    project(shard)
    part[...] += stream_ref[...].astype(jnp.float32)

    @pl.when(shard > 0)
    def _():
        sum_copy(0, shard, 0).wait_recv()
        part[...] += sums_in[0, shard].astype(jnp.float32)

    @pl.when(shard < last)
    def _():
        sum_copy(1, shard, 0).wait_recv()
        part[...] += sums_in[1, shard].astype(jnp.float32)

    out_ref[...] = part[...].astype(jnp.bfloat16)

    def drain(dest, carry):
        @pl.when(dest > shard)
        def _():
            sum_copy(0, dest, 0).wait_send()

        @pl.when(dest < shard)
        def _():
            sum_copy(1, dest, 0).wait_send()

        return carry

    lax.fori_loop(0, chan_size, drain, 0)


def mix(seq_size, chan_size, proj, stream, short_filter, decay_rate, residue, skip_gain, out_weight):
    rows, channels = stream.shape
    modes = decay_rate.shape[0]
    groups = channels // LANES
    f32, bf16 = jnp.float32, jnp.bfloat16
    vmem = pl.BlockSpec(memory_space=pltpu.VMEM)
    dma = pltpu.SemaphoreType.DMA
    return pl.pallas_call(
        functools.partial(block_kernel, seq_size, chan_size),
        out_shape=jax.ShapeDtypeStruct((rows, channels), bf16),
        in_specs=[vmem] * 6 + [pl.BlockSpec(memory_space=pl.ANY)],
        out_specs=vmem,
        scratch_shapes=[
            pltpu.VMEM((chan_size, channels, channels), bf16),
            pltpu.VMEM((FEAT, 8, channels), f32),
            pltpu.VMEM((FEAT, 8, channels), f32),
            pltpu.VMEM((FEAT, rows + 8, LANES), f32),
            pltpu.VMEM((groups, rows, LANES), f32),
            pltpu.VMEM((groups, rows, LANES), f32),
            pltpu.VMEM((groups, modes, SEGS, LANES), f32),
            pltpu.VMEM((modes, channels), f32),
            pltpu.VMEM((seq_size, modes, channels), f32),
            pltpu.VMEM((modes, channels), f32),
            pltpu.VMEM((modes, SEGS, LANES), f32),
            pltpu.VMEM((rows, LANES), f32),
            pltpu.VMEM((rows, channels), bf16),
            pltpu.VMEM((rows, channels), f32),
            pltpu.VMEM((2, chan_size, rows, channels), bf16),
            pltpu.VMEM((2, chan_size, rows, channels), bf16),
            dma((chan_size,)),
            dma((2,)),
            dma((seq_size,)),
            dma((seq_size,)),
            dma((2, chan_size)),
            dma((2, chan_size)),
        ],
        compiler_params=pltpu.CompilerParams(
            collective_id=0, has_side_effects=True, vmem_limit_bytes=48 << 20
        ),
    )(
        proj,
        stream,
        short_filter.reshape(FEAT * FEAT, channels),
        decay_rate,
        residue,
        skip_gain.reshape(1, channels),
        out_weight,
    )


def on_device(
    seq_size,
    chan_size,
    tokens,
    embedding,
    norm_gain,
    in_weight,
    short_filter,
    decay_rate,
    residue,
    skip_gain,
    out_weight,
):
    vocab_size = embedding.shape[0]
    one_hot = (tokens[:, None] == jnp.arange(vocab_size, dtype=jnp.int32)[None, :]).astype(
        jnp.bfloat16
    )
    stream = jnp.dot(one_hot, embedding, preferred_element_type=jnp.float32).astype(jnp.bfloat16)
    gathered = lax.all_gather(stream, "chan", axis=1, tiled=True)
    gathered_f = gathered.astype(jnp.float32)
    scale = lax.rsqrt(jnp.mean(gathered_f * gathered_f, axis=1, keepdims=True) + 1e-06)
    normed = (gathered_f * scale * norm_gain[None, :]).astype(jnp.bfloat16)
    proj = jnp.einsum("td,djc->jtc", normed, in_weight, preferred_element_type=jnp.float32).astype(
        jnp.bfloat16
    )
    return mix(
        seq_size, chan_size, proj, stream, short_filter, decay_rate, residue, skip_gain, out_weight
    )


def solution(mesh):
    placed = (
        P("seq"),
        P(None, "chan"),
        P(),
        P(None, None, "chan"),
        P(None, None, "chan"),
        P(None, "chan"),
        P(None, "chan"),
        P("chan"),
        P("chan", None),
    )
    return jax.shard_map(
        functools.partial(on_device, mesh.shape["seq"], mesh.shape["chan"]),
        mesh=mesh,
        in_specs=placed,
        out_specs=P("seq", "chan"),
        check_vma=False,
    )
```

time: 485 us -> 141 us (0.29)
  local copies, waits for them, and re-layouts: 154 us -> 2.86 us
  matrix products: 165 us -> 14.3 us
  Pallas kernels: 0 us -> 59.8 us
  waiting for transfers between devices: 99.3 us -> 48 us
  other arithmetic: 25.9 us -> 2.09 us
  blocking collectives: 22.6 us -> 0 us
    dot_general x5 -> x1, matrix products: 163 us -> 12.3 us  [on_device(): jnp.einsum('td,djc->jtc', normed, in_weight, preferred_element_type=jnp.f...]
    gather x2 -> x0, local copies, waits for them, and re-layouts: 141 us -> none  [on_device(): impulse[jnp.clip(lag_table, 0, BLK - 1)]]
    reduce_scatter x1 -> x0, waiting for transfers between devices: 81 us -> none  [on_device(): lax.psum_scatter(lax.dot_general(out_weight, hidden, (((0,), (1,)), ((),...]
    pallas_call x0 -> x1, Pallas kernels: none -> 59.8 us  [mix(): pl.pallas_call(functools.partial(block_kernel, seq_size, chan_size), out_...]
    all_gather x1, waiting for transfers between devices: 18.3 us -> 48 us  [on_device(): gathered = lax.all_gather(stream, 'chan', axis=1, tiled=True)]
    all_gather x2 -> x0, blocking collectives: 22.6 us -> none  [carried_in(): gathered = jax.tree.map(lambda a: lax.all_gather(a, axis), part)]
    reduce_sum x1 -> x0, other arithmetic: 11.7 us -> none  [on_device(): jnp.sum(residue[:, None, :] * jnp.exp(-decay_rate[:, None, :] * steps_f[N...]
    convert_element_type x7 -> x0, other arithmetic: 7.63 us -> none  [the longest x1 2.16 us: on_device(): return (stream.astype(jnp.float32) + mixed).astype(jnp.bfloat16)]
  transfers between devices with their start and end apart: 3 -> 1, of which waited for: 2 -> 1; matrix products, arithmetic and copies ran while one was open for 33% -> 1% of each run, Pallas kernels for 0% -> 0%
where the time goes in v1:
time: 141 us; the launch traced here: 140 us
  Pallas kernels  59.8 us (42%)
  waiting for transfers between devices  48 us (34%)
  matrix products  14.3 us (10%)
  between operations  13.5 us (10%)
  local copies, waits for them, and re-layouts  2.86 us (2%)
  other arithmetic  2.09 us (1%)
    pallas_call x1, Pallas kernels, mix(): pl.pallas_call(functools.partial(block_kernel, seq_size, chan_size), out_...  59.8 us
    all_gather x1, waiting for transfers between devices, on_device(): gathered = lax.all_gather(stream, 'chan', axis=1, tiled=True)  48 us
    dot_general x1, matrix products, on_device(): jnp.einsum('td,djc->jtc', normed, in_weight, preferred_element_type=jnp.f...  12.3 us
  transfers between devices with their start and end apart: 1, of which 1 were waited for; matrix products, arithmetic and copies ran while one was open for 1% of the time, Pallas kernels for 0%

profile of v1, /device:TPU:0, one launch (start us, length us, event | category | flops | bytes accessed | tf_op | source)
XLA Modules:
  0.0 140.4 jit_solution(6805309058372397030)
XLA Ops:
  6.5 0.0 copy-start
  6.5 0.0 copy-start.5
  6.5 0.0 all-gather.2.cloned.1.call-start
  6.5 1.2 copy-done
  7.8 2.0 %convolution_convert_fusion.stream_ref = bf16[256,1024]{1,0:T(8,128)(2,1)} fusion(bf16[512,1024]{1,0:T(8,128)(2,1)S(1)} %copy-done, s32[256]{0:T(256)} %param.9), kind=kOutput, calls=%fused_computation.11 | convolution fusion | flops 268828672 | bytes 1573888 | tf_op jit(solution)/shard_map/dot_general | solution.py:333
  9.7 0.0 all-gather.2.cloned.1.call-update
  9.7 0.8 reshape.16.filter_ref
  10.6 48.0 %all-gather.2.cloned.1.call-done = bf16[256,4096]{1,0:T(8,128)(2,1)} async-done(((bf16[256,1024]{1,0:T(8,128)(2,1)}), bf16[256,4096]{1,0:T(8,128)(2,1)}) %all-gather.2.cloned.1.call-update) | async-done | bytes 2097168 | tf_op jit(solution)/shard_map/all_gather | solution.py:334
  58.5 2.1 %fusion = f32[256]{0:T(256)S(1)} fusion(bf16[256,4096]{1,0:T(8,128)(2,1)} %all-gather.2.cloned.1.call-done), kind=kLoop, calls=%fused_computation.2 | loop fusion | flops 3145472 | bytes 2098176 | tf_op jit(solution)/shard_map/reduce_sum | solution.py:336
  60.6 0.0 copy-done.5
  60.6 0.0 copy-start.1
  60.7 0.0 copy-start.2
  60.7 0.0 copy-start.3
  60.7 0.0 copy-start.4
  60.7 12.3 %fusion.11.proj_ref = bf16[3,256,1024]{2,1,0:T(8,128)(2,1)S(1)} fusion(bf16[4096,3,1024]{2,0,1:T(8,128)(2,1)} %param.12, bf16[256,4096]{1,0:T(8,128)(2,1)} %all-gather.2.cloned.1.call-done, f32[4096]{0:T(1024)S(1)} %copy-done.5, f32[256]{0:T(256)S(1)} %add_rsqrt_fusion), kind=kOutput, calls=%fused_computation.10 | convolution fusion | flops 6447431680 | bytes 28853248 | tf_op jit(solution)/shard_map/td,djc->jtc/dot_general | solution.py:338
  73.0 0.0 copy-done.1
  73.0 0.0 copy-done.2
  73.0 0.0 copy-done.3
  73.0 0.0 copy-done.4
  73.0 59.8 %shard_map.91 = bf16[256,1024]{1,0:T(8,128)(2,1)S(1)} custom-call(bf16[3,256,1024]{2,1,0:T(8,128)(2,1)S(1)} %fusion.11.proj_ref, bf16[256,1024]{1,0:T(8,128)(2,1)S(1)} %copy-done.1, f32[9,1024]{1,0:T(8,128)S(1)} %reshape.16.filter_ref, f32[16,1024]{1,0:T(8,128)S(1)} %copy-done.2, f32[16,1024]{1,0:T(8,128)S(1)} %copy-done.3, f32[1,1024]{1,0:T(1,128)S(1)} %bitcast.12, ...), custom_call_target="tpu_custom_call" | custom-call | tf_op jit(solution)/shard_map/pallas_call | solution.py:273
  132.8 0.8 copy.11
  (1 shorter events, 0.0 us)
Async XLA Ops:
  6.5 1.2 copy-start
  6.5 54.1 %copy-start.5 = (f32[4096]{0:T(1024)S(1)}, f32[4096]{0:T(1024)}, u32[]{:S(2)}) copy-start(f32[4096]{0:T(1024)} %param.11) | copy-start | bytes 49156
  6.5 52.0 %all-gather.2.cloned.1.call-start = ((), (), s32[]{:S(2)}) async-start(), calls=%async_computation | async-start | bytes 2621440 | tf_op jit(solution)/shard_map/all_gather | solution.py:334
  60.6 12.4 %copy-start.1 = (bf16[256,1024]{1,0:T(8,128)(2,1)S(1)}, bf16[256,1024]{1,0:T(8,128)(2,1)}, u32[]{:S(2)}) copy-start(bf16[256,1024]{1,0:T(8,128)(2,1)} %convolution_convert_fusion.stream_ref) | copy-start | bytes 1572868
  60.7 12.4 %copy-start.2 = (f32[16,1024]{1,0:T(8,128)S(1)}, f32[16,1024]{1,0:T(8,128)}, u32[]{:S(2)}) copy-start(f32[16,1024]{1,0:T(8,128)} %decay_ref.1) | copy-start | bytes 196612
  60.7 12.4 %copy-start.3 = (f32[16,1024]{1,0:T(8,128)S(1)}, f32[16,1024]{1,0:T(8,128)}, u32[]{:S(2)}) copy-start(f32[16,1024]{1,0:T(8,128)} %residue_ref.1) | copy-start | bytes 196612
  60.7 12.4 %copy-start.4 = (f32[1024]{0:T(1024)S(1)}, f32[1024]{0:T(1024)}, u32[]{:S(2)}) copy-start(f32[1024]{0:T(1024)} %param.16) | copy-start | bytes 12292
Sparse Core Ops, SparseCore 0:
  9.9 48.6 all-gather.1

commit v2 on v1

--- a/solution.py
+++ b/solution.py
@@ -16,15 +16,23 @@
 def block_kernel(
     seq_size,
     chan_size,
-    proj_ref,
-    stream_ref,
+    tokens_ref,
+    embed_ref,
+    norm_ref,
     filter_ref,
     decay_ref,
     residue_ref,
     skip_ref,
+    in_weight_ref,
     weight_ref,
     out_ref,
+    in_buf,
     weight_buf,
+    gathered,
+    squares_out,
+    squares_in,
+    normed,
+    proj,
     rim_out,
     rim_in,
     padded,
@@ -40,7 +48,12 @@
     part,
     sums_out,
     sums_in,
+    in_sem,
     weight_sem,
+    square_send_sem,
+    square_recv_sem,
+    gather_send_sem,
+    gather_recv_sem,
     rim_sem,
     end_send_sem,
     end_recv_sem,
@@ -49,11 +62,29 @@
 ):
     place = lax.axis_index("seq")
     shard = lax.axis_index("chan")
-    rows, channels = stream_ref.shape
+    last = chan_size - 1
+    rows = tokens_ref.shape[1]
+    vocab, channels = embed_ref.shape
     modes = decay_ref.shape[0]
     groups = channels // LANES
     seg = rows // SEGS
-
+    tile = min(256, channels)
+    tiles = channels // tile
+
+    def in_copy(d, j):
+        depth = pl.ds(pl.multiple_of(d * channels, channels), channels)
+        return pltpu.make_async_copy(
+            in_weight_ref.at[j, depth, :], in_buf.at[d, j], in_sem.at[d, j]
+        )
+
+    def start_in(d):
+        for j in range(FEAT):
+            in_copy(d, j).start()
+
+    start_in(shard)
+    for k in range(1, chan_size):
+        pl.when(shard - k >= 0)(functools.partial(start_in, shard - k))
+        pl.when(shard + k <= last)(functools.partial(start_in, shard + k))
     weight_copies = [
         pltpu.make_async_copy(
             weight_ref.at[:, pl.ds(d * channels, channels)], weight_buf.at[d], weight_sem.at[d]
@@ -72,10 +103,110 @@
         pl.semaphore_signal(
             barrier, 1, device_id={"chan": lax.rem(shard + k, chan_size)}, device_id_type=MESH
         )
+    ids = lax.broadcasted_iota(jnp.int32, (vocab, rows), 0)
+    one_hot = (ids == tokens_ref[...]).astype(jnp.float32).astype(jnp.bfloat16)
+    stream = lax.dot_general(
+        one_hot, embed_ref[...], (((0,), (0,)), ((), ())), preferred_element_type=jnp.float32
+    )
+    gathered[shard] = stream.astype(jnp.bfloat16)
+    ones = jnp.ones((8, channels), jnp.float32)
+    squares_out[...] = lax.dot_general(
+        ones,
+        stream * stream,
+        (((1,), (1,)), ((), ())),
+        precision=lax.Precision.HIGHEST,
+        preferred_element_type=jnp.float32,
+    )
+    pl.semaphore_wait(barrier, seq_size - 1 + chan_size - 1)
+
+    def square_copy(to, source):
+        return pltpu.make_async_remote_copy(
+            src_ref=squares_out,
+            dst_ref=squares_in.at[source],
+            send_sem=square_send_sem.at[to],
+            recv_sem=square_recv_sem.at[source],
+            device_id={"chan": to},
+            device_id_type=MESH,
+        )
+
+    def gather_copy(way, which, to):
+        return pltpu.make_async_remote_copy(
+            src_ref=gathered.at[which],
+            dst_ref=gathered.at[which],
+            send_sem=gather_send_sem.at[way, which],
+            recv_sem=gather_recv_sem.at[which],
+            device_id={"chan": to},
+            device_id_type=MESH,
+        )
+
+    for k in range(1, chan_size):
+        square_copy(lax.rem(shard + k, chan_size), shard).start()
+
+    def send_up(which):
+        @pl.when(shard < last)
+        def _():
+            gather_copy(0, which, shard + 1).start()
+
+    def send_down(which):
+        @pl.when(shard > 0)
+        def _():
+            gather_copy(1, which, shard - 1).start()
+
+    send_up(shard)
+    send_down(shard)
+    proj[...] = jnp.zeros_like(proj)
+    total = squares_out[...]
+    for k in range(1, chan_size):
+        peer = lax.rem(shard + k, chan_size)
+        square_copy(peer, shard).wait_send()
+        square_copy(peer, peer).wait_recv()
+        total = total + squares_in[peer]
+    scale = lax.rsqrt(total.T[:, :1] * (1.0 / (channels * chan_size)) + 1e-06)
+
+    def absorb(which):
+        for j in range(FEAT):
+            in_copy(which, j).wait()
+        cols = pl.ds(pl.multiple_of(which * channels, channels), channels)
+        normed[...] = (gathered[which].astype(jnp.float32) * scale * norm_ref[:, cols]).astype(
+            jnp.bfloat16
+        )
+
+        def one(t, carry):
+            j = t // tiles
+            at = pl.ds(pl.multiple_of((t % tiles) * tile, tile), tile)
+            proj[j, :, at] += jnp.dot(
+                normed[...], in_buf[which, j, :, at], preferred_element_type=jnp.float32
+            )
+            return carry
+
+        lax.fori_loop(0, FEAT * tiles, one, 0)
+
+    absorb(shard)
+
+    def gather_step(k, carry):
+        below, above = shard - k, shard + k
+
+        @pl.when(below >= 0)
+        def _():
+            gather_copy(0, below, 0).wait_recv()
+            send_up(below)
+
+        @pl.when(above <= last)
+        def _():
+            gather_copy(1, above, 0).wait_recv()
+            send_down(above)
+
+        pl.when(below >= 0)(functools.partial(absorb, below))
+        pl.when(above <= last)(functools.partial(absorb, above))
+        return carry
+
+    lax.fori_loop(1, chan_size, gather_step, 0)
+
+    def rounded(value):
+        return value.astype(jnp.bfloat16).astype(jnp.float32)
+
     for j in range(FEAT):
-        rim_out[j] = proj_ref[j, rows - 16 :, :].astype(jnp.float32)[8:]
-    pl.semaphore_wait(barrier, seq_size - 1 + chan_size - 1)
-
+        rim_out[j] = rounded(proj[j, rows - 8 :, :])
     rim_copy = pltpu.make_async_remote_copy(
         src_ref=rim_out,
         dst_ref=rim_in,
@@ -95,14 +226,16 @@
         lanes = pl.ds(pl.multiple_of(g * LANES, LANES), LANES)
         feat = []
         for j in range(FEAT):
-            now = proj_ref[j, :, lanes].astype(jnp.float32)
+            now = rounded(proj[j, :, lanes])
             padded[j, 8:, :] = now
             padded[j, :8, :] = rim_in[j, :, lanes] * keep
-            total = filter_ref[j : j + 1, lanes] * now
+            total = filter_ref[0, j : j + 1, lanes] * now
             for offset in range(1, FEAT):
-                row = offset * FEAT + j
-                total = total + filter_ref[row : row + 1, lanes] * padded[j, pl.ds(8 - offset, rows), :]
-            feat.append(total.astype(jnp.bfloat16).astype(jnp.float32))
+                total = (
+                    total
+                    + filter_ref[offset, j : j + 1, lanes] * padded[j, pl.ds(8 - offset, rows), :]
+                )
+            feat.append(rounded(total))
         query_buf[g] = feat[0]
         driven_buf[g] = feat[1] * feat[2]
         decay = decay_ref[:, lanes]
@@ -123,31 +256,26 @@
         own_end[:, lanes] = end
         return carry
 
-    lax.fori_loop(0, groups, first_pass, 0)
-
-    def end_copy(to, source):
+    halves = 2 if groups > 1 else 1
+    width = channels // halves
+    per_half = groups // halves
+
+    def end_copy(half, to, source):
+        cols = pl.ds(half * width, width)
         return pltpu.make_async_remote_copy(
-            src_ref=own_end,
-            dst_ref=all_ends.at[source],
-            send_sem=end_send_sem.at[to],
-            recv_sem=end_recv_sem.at[source],
+            src_ref=own_end.at[:, cols],
+            dst_ref=all_ends.at[source, :, cols],
+            send_sem=end_send_sem.at[half, to],
+            recv_sem=end_recv_sem.at[half, source],
             device_id={"seq": to},
             device_id_type=MESH,
         )
 
-    for k in range(1, seq_size):
-        end_copy(lax.rem(place + k, seq_size), place).start()
-    for k in range(1, seq_size):
-        peer = lax.rem(place + k, seq_size)
-        end_copy(peer, place).wait_send()
-        end_copy(peer, peer).wait_recv()
+    for half in range(halves):
+        lax.fori_loop(half * per_half, (half + 1) * per_half, first_pass, 0)
+        for k in range(1, seq_size):
+            end_copy(half, lax.rem(place + k, seq_size), place).start()
     all_ends[place] = own_end[...]
-
-    span = jnp.exp(-decay_ref[...] * rows)
-    state = jnp.zeros((modes, channels), jnp.float32)
-    for p in range(seq_size - 1):
-        state = jnp.where(p < place, span * state + all_ends[p], state)
-    incoming[...] = state
 
     def second_pass(g, carry):
         lanes = pl.ds(pl.multiple_of(g * LANES, LANES), LANES)
@@ -173,11 +301,20 @@
         hidden[:, lanes] = hidden_f[...].astype(jnp.bfloat16)
         return carry
 
-    lax.fori_loop(0, groups, second_pass, 0)
+    for half in range(halves):
+        for k in range(1, seq_size):
+            peer = lax.rem(place + k, seq_size)
+            end_copy(half, peer, place).wait_send()
+            end_copy(half, peer, peer).wait_recv()
+        cols = slice(half * width, (half + 1) * width)
+        span = jnp.exp(-decay_ref[:, cols] * rows)
+        state = jnp.zeros((modes, width), jnp.float32)
+        for p in range(seq_size - 1):
+            state = jnp.where(p < place, span * state + all_ends[p, :, cols], state)
+        incoming[:, cols] = state
+        lax.fori_loop(half * per_half, (half + 1) * per_half, second_pass, 0)
     for copy in weight_copies:
         copy.wait()
-
-    tile = min(256, channels)
 
     def project(dest):
         def one(t, carry):
@@ -187,7 +324,7 @@
             )
             return carry
 
-        lax.fori_loop(0, channels // tile, one, 0)
+        lax.fori_loop(0, tiles, one, 0)
 
     def sum_copy(way, dest, to):
         return pltpu.make_async_remote_copy(
@@ -199,8 +336,6 @@
             device_id_type=MESH,
         )
 
-    last = chan_size - 1
-
     def pass_on(way, dest, to, has_earlier):
         project(dest)
 
@@ -235,7 +370,7 @@
     lax.fori_loop(0, 2 * last, sum_step, 0)
 
     project(shard)
-    part[...] += stream_ref[...].astype(jnp.float32)
+    part[...] += gathered[shard].astype(jnp.float32)
 
     @pl.when(shard > 0)
     def _():
@@ -258,25 +393,53 @@
         def _():
             sum_copy(1, dest, 0).wait_send()
 
+        @pl.when((dest <= shard) & (shard < last))
+        def _():
+            gather_copy(0, dest, 0).wait_send()
+
+        @pl.when((dest >= shard) & (shard > 0))
+        def _():
+            gather_copy(1, dest, 0).wait_send()
+
         return carry
 
     lax.fori_loop(0, chan_size, drain, 0)
 
 
-def mix(seq_size, chan_size, proj, stream, short_filter, decay_rate, residue, skip_gain, out_weight):
-    rows, channels = stream.shape
+def on_device(
+    seq_size,
+    chan_size,
+    tokens,
+    embedding,
+    norm_gain,
+    in_weight,
+    short_filter,
+    decay_rate,
+    residue,
+    skip_gain,
+    out_weight,
+):
+    rows = tokens.shape[0]
+    channels = embedding.shape[1]
     modes = decay_rate.shape[0]
     groups = channels // LANES
     f32, bf16 = jnp.float32, jnp.bfloat16
     vmem = pl.BlockSpec(memory_space=pltpu.VMEM)
+    hbm = pl.BlockSpec(memory_space=pl.ANY)
     dma = pltpu.SemaphoreType.DMA
     return pl.pallas_call(
         functools.partial(block_kernel, seq_size, chan_size),
         out_shape=jax.ShapeDtypeStruct((rows, channels), bf16),
-        in_specs=[vmem] * 6 + [pl.BlockSpec(memory_space=pl.ANY)],
+        in_specs=[vmem] * 7 + [hbm] * 2,
         out_specs=vmem,
         scratch_shapes=[
+            pltpu.VMEM((chan_size, FEAT, channels, channels), bf16),
             pltpu.VMEM((chan_size, channels, channels), bf16),
+            pltpu.VMEM((chan_size, rows, channels), bf16),
+            pltpu.VMEM((8, rows), f32),
+            pltpu.VMEM((chan_size, 8, rows), f32),
+            pltpu.VMEM((rows, channels), bf16),
+            pltpu.VMEM((FEAT, rows, channels), f32),
             pltpu.VMEM((FEAT, 8, channels), f32),
             pltpu.VMEM((FEAT, 8, channels), f32),
             pltpu.VMEM((FEAT, rows + 8, LANES), f32),
@@ -292,54 +455,31 @@
             pltpu.VMEM((rows, channels), f32),
             pltpu.VMEM((2, chan_size, rows, channels), bf16),
             pltpu.VMEM((2, chan_size, rows, channels), bf16),
+            dma((chan_size, FEAT)),
+            dma((chan_size,)),
+            dma((chan_size,)),
+            dma((chan_size,)),
+            dma((2, chan_size)),
             dma((chan_size,)),
             dma((2,)),
-            dma((seq_size,)),
-            dma((seq_size,)),
+            dma((2, seq_size)),
+            dma((2, seq_size)),
             dma((2, chan_size)),
             dma((2, chan_size)),
         ],
         compiler_params=pltpu.CompilerParams(
-            collective_id=0, has_side_effects=True, vmem_limit_bytes=48 << 20
+            collective_id=0, has_side_effects=True, vmem_limit_bytes=60 << 20
         ),
     )(
-        proj,
-        stream,
-        short_filter.reshape(FEAT * FEAT, channels),
+        tokens.reshape(1, rows),
+        embedding,
+        norm_gain.reshape(1, -1),
+        short_filter,
         decay_rate,
         residue,
         skip_gain.reshape(1, channels),
+        in_weight.transpose(1, 0, 2),
         out_weight,
-    )
-
-
-def on_device(
-    seq_size,
-    chan_size,
-    tokens,
-    embedding,
-    norm_gain,
-    in_weight,
-    short_filter,
-    decay_rate,
-    residue,
-    skip_gain,
-    out_weight,
-):
-    vocab_size = embedding.shape[0]
-    one_hot = (tokens[:, None] == jnp.arange(vocab_size, dtype=jnp.int32)[None, :]).astype(
-        jnp.bfloat16
-    )
-    stream = jnp.dot(one_hot, embedding, preferred_element_type=jnp.float32).astype(jnp.bfloat16)
-    gathered = lax.all_gather(stream, "chan", axis=1, tiled=True)
-    gathered_f = gathered.astype(jnp.float32)
-    scale = lax.rsqrt(jnp.mean(gathered_f * gathered_f, axis=1, keepdims=True) + 1e-06)
-    normed = (gathered_f * scale * norm_gain[None, :]).astype(jnp.bfloat16)
-    proj = jnp.einsum("td,djc->jtc", normed, in_weight, preferred_element_type=jnp.float32).astype(
-        jnp.bfloat16
-    )
-    return mix(
-        seq_size, chan_size, proj, stream, short_filter, decay_rate, residue, skip_gain, out_weight
     )
 
 

time: 141 us -> 106 us (0.75)
  waiting for transfers between devices: 48 us -> 0 us
  Pallas kernels: 59.8 us -> 104 us
  matrix products: 14.3 us -> 0 us
  between operations: 13.5 us -> 0.01 us
  other arithmetic: 2.09 us -> 0 us
    all_gather x1 -> x0, waiting for transfers between devices: 48 us -> none  [on_device(): gathered = lax.all_gather(stream, 'chan', axis=1, tiled=True)]
    pallas_call x1, Pallas kernels: 59.8 us -> 104 us  [on_device(): pl.pallas_call(functools.partial(block_kernel, seq_size, chan_size), out_...]
    dot_general x2 -> x0, matrix products: 14.3 us -> none  [the longest x1 12.3 us: on_device(): jnp.einsum('td,djc->jtc', normed, in_weight, preferred_element_type=jnp.f...]
    reduce_sum x1 -> x0, other arithmetic: 2.08 us -> none  [on_device(): jnp.mean(gathered_f * gathered_f, axis=1, keepdims=True) + 1e-06]
  transfers between devices with their start and end apart: 1 -> 0, of which waited for: 1 -> 0; matrix products, arithmetic and copies ran while one was open for 1% -> 0% of each run, Pallas kernels for 0% -> 0%
where the time goes in v2:
time: 106 us
  Pallas kernels  104 us (98%)
  local copies, waits for them, and re-layouts  1.87 us (2%)
    pallas_call x1, Pallas kernels, on_device(): pl.pallas_call(functools.partial(block_kernel, seq_size, chan_size), out_...  104 us

profile of v2, /device:TPU:0, one launch (start us, length us, event | category | flops | bytes accessed | tf_op | source)
XLA Modules:
  0.0 106.2 jit_solution(17598980800458345324)
XLA Ops:
  0.0 104.4 %shard_map.91 = bf16[256,1024]{1,0:T(8,128)(2,1)} custom-call(s32[1,256]{1,0:T(1,128)} %bitcast.7, bf16[512,1024]{1,0:T(8,128)(2,1)} %embed_ref.1, f32[1,4096]{1,0:T(1,128)} %bitcast.5, f32[3,3,1024]{2,1,0:T(4,128)} %filter_ref.1, f32[16,1024]{1,0:T(8,128)} %decay_ref.1, f32[16,1024]{1,0:T(8,128)} %residue_ref.1, f32[1,1024]{1,0:T(1,128)} %bitcast.6, ...), custom_call_target="tpu_custom_call" | custom-call | tf_op jit(solution)/shard_map/pallas_call | solution.py:430
  104.4 1.9 %copy.11 = bf16[256,1024]{1,0:T(8,128)(2,1)} copy(bf16[256,1024]{1,0:T(8,128)(2,1)} %shard_map.91) | data formatting | bytes 1048576

commit v3 on v2

v3 whole, which is shorter than its diff:
```python
import functools

import jax
import jax.numpy as jnp
from jax import lax
from jax.experimental import pallas as pl
from jax.experimental.pallas import tpu as pltpu
from jax.sharding import PartitionSpec as P

FEAT = 3
LANES = 128
SEGS = 8
MESH = pl.DeviceIdType.MESH


def block_kernel(
    seq_size,
    chan_size,
    tokens_ref,
    embed_ref,
    norm_ref,
    filter_ref,
    decay_ref,
    residue_ref,
    skip_ref,
    in_weight_ref,
    weight_ref,
    out_ref,
    in_buf,
    weight_buf,
    tokens_in,
    gathered,
    squares_out,
    squares_in,
    normed,
    proj,
    rim_out,
    rim_in,
    padded,
    query_buf,
    driven_buf,
    seg_ends,
    own_end,
    all_ends,
    incoming,
    seg_starts,
    hidden_f,
    hidden,
    part,
    sums_out,
    sums_in,
    result_out,
    result_in,
    in_sem,
    weight_sem,
    token_send_sem,
    token_recv_sem,
    square_send_sem,
    square_recv_sem,
    gather_send_sem,
    gather_recv_sem,
    rim_send_sem,
    rim_recv_sem,
    end_send_sem,
    end_recv_sem,
    sum_send_sem,
    sum_recv_sem,
    result_send_sem,
    result_recv_sem,
):
    place = lax.axis_index("seq")
    shard = lax.axis_index("chan")
    last = chan_size - 1
    rows = tokens_ref.shape[2]
    vocab, channels = embed_ref.shape
    modes = decay_ref.shape[0]
    groups = channels // LANES
    seg = rows // SEGS
    tile = min(256, channels)
    tiles = channels // tile
    inner = (shard > 0) & (shard < last)
    outer = jnp.logical_not(inner)

    def in_copy(d, j):
        depth = pl.ds(pl.multiple_of(d * channels, channels), channels)
        return pltpu.make_async_copy(
            in_weight_ref.at[j, depth, :], in_buf.at[d, j], in_sem.at[d, j]
        )

    def start_in(d):
        for j in range(FEAT):
            in_copy(d, j).start()

    barrier = pltpu.get_barrier_semaphore()
    for k in range(1, seq_size):
        pl.semaphore_signal(
            barrier, 1, device_id={"seq": lax.rem(place + k, seq_size)}, device_id_type=MESH
        )
    for k in range(1, chan_size):
        pl.semaphore_signal(
            barrier, 1, device_id={"chan": lax.rem(shard + k, chan_size)}, device_id_type=MESH
        )

    start_in(shard)
    for k in range(1, chan_size):
        pl.when(shard - k >= 0)(functools.partial(start_in, shard - k))
        pl.when(shard + k <= last)(functools.partial(start_in, shard + k))
    weight_copies = [
        pltpu.make_async_copy(
            weight_ref.at[:, pl.ds(d * channels, channels)], weight_buf.at[d], weight_sem.at[d]
        )
        for d in range(chan_size)
    ]
    for copy in weight_copies:
        copy.start()
    pl.semaphore_wait(barrier, seq_size - 1 + chan_size - 1)

    def token_copy(half, phase, to):
        return pltpu.make_async_remote_copy(
            src_ref=tokens_ref.at[half],
            dst_ref=tokens_in.at[phase],
            send_sem=token_send_sem.at[half],
            recv_sem=token_recv_sem.at[phase],
            device_id={"seq": to},
            device_id_type=MESH,
        )

    for half in range(2):
        block = 2 * place + half
        phase, to = block // seq_size, lax.rem(block, seq_size)

        @pl.when(to != place)
        def _():
            token_copy(half, phase, to).start()

        @pl.when(to == place)
        def _():
            tokens_in[phase] = tokens_ref[half]

    def square_copy(h, to, source):
        return pltpu.make_async_remote_copy(
            src_ref=squares_out.at[h],
            dst_ref=squares_in.at[h, source],
            send_sem=square_send_sem.at[h, to],
            recv_sem=square_recv_sem.at[h, source],
            device_id={"chan": to},
            device_id_type=MESH,
        )

    def gather_copy(h, way, which, to):
        return pltpu.make_async_remote_copy(
            src_ref=gathered.at[h, which],
            dst_ref=gathered.at[h, which],
            send_sem=gather_send_sem.at[h, way, which],
            recv_sem=gather_recv_sem.at[h, which],
            device_id={"chan": to},
            device_id_type=MESH,
        )

    def send_up(h, which):
        @pl.when(shard < last)
        def _():
            gather_copy(h, 0, which, shard + 1).start()

    def send_down(h, which):
        @pl.when(shard > 0)
        def _():
            gather_copy(h, 1, which, shard - 1).start()

    def send_own(h):
        send_up(h, shard)
        send_down(h, shard)

    def look_up(h):
        source = (h * seq_size + place) // 2

        @pl.when(source != place)
        def _():
            token_copy(0, h, 0).wait_recv()

        ids = lax.broadcasted_iota(jnp.int32, (vocab, rows), 0)
        one_hot = (ids == tokens_in[h]).astype(jnp.float32).astype(jnp.bfloat16)
        stream = lax.dot_general(
            one_hot, embed_ref[...], (((0,), (0,)), ((), ())), preferred_element_type=jnp.float32
        )
        gathered[h, shard] = stream.astype(jnp.bfloat16)
        return stream

    def send_squares(h, stream):
        squares_out[h] = lax.dot_general(
            jnp.ones((8, channels), jnp.float32),
            stream * stream,
            (((1,), (1,)), ((), ())),
            precision=lax.Precision.HIGHEST,
            preferred_element_type=jnp.float32,
        )
        for k in range(1, chan_size):
            square_copy(h, lax.rem(shard + k, chan_size), shard).start()

    first = look_up(0)
    send_own(0)
    send_squares(0, first)
    second = look_up(1)
    pl.when(outer)(functools.partial(send_own, 1))
    send_squares(1, second)

    def row_scale(h):
        total = squares_out[h]
        for k in range(1, chan_size):
            peer = lax.rem(shard + k, chan_size)
            square_copy(h, peer, shard).wait_send()
            square_copy(h, peer, peer).wait_recv()
            total = total + squares_in[h, peer]
        return lax.rsqrt(total.T[:, :1] * (1.0 / (channels * chan_size)) + 1e-06)

    def gather(h):
        proj[...] = jnp.zeros_like(proj)
        scale = row_scale(h)

        def absorb(which):
            if h == 0:
                for j in range(FEAT):
                    in_copy(which, j).wait()
            cols = pl.ds(pl.multiple_of(which * channels, channels), channels)
            normed[...] = (
                gathered[h, which].astype(jnp.float32) * scale * norm_ref[:, cols]
            ).astype(jnp.bfloat16)

            def one(t, carry):
                j = t // tiles
                at = pl.ds(pl.multiple_of((t % tiles) * tile, tile), tile)
                proj[j, :, at] += jnp.dot(
                    normed[...], in_buf[which, j, :, at], preferred_element_type=jnp.float32
                )
                return carry

            lax.fori_loop(0, FEAT * tiles, one, 0)

        if h == 0:
            absorb(shard)
        else:
            pl.when(outer)(functools.partial(absorb, shard))

        def gather_step(k, carry):
            below, above = shard - k, shard + k

            @pl.when(below >= 0)
            def _():
                gather_copy(h, 0, below, 0).wait_recv()
                send_up(h, below)

            @pl.when(above <= last)
            def _():
                gather_copy(h, 1, above, 0).wait_recv()
                send_down(h, above)

            pl.when(below >= 0)(functools.partial(absorb, below))
            pl.when(above <= last)(functools.partial(absorb, above))
            return carry

        lax.fori_loop(1, chan_size, gather_step, 0)
        if h == 1:
            pl.when(inner)(functools.partial(absorb, shard))

    def rounded(value):
        return value.astype(jnp.bfloat16).astype(jnp.float32)

    def spread(value):
        return jnp.broadcast_to(value[:, None, :], (value.shape[0], SEGS, LANES))

    halves = 2 if groups > 1 else 1
    width = channels // halves
    per_half = groups // halves

    def middle(h):
        for j in range(FEAT):
            rim_out[h, j] = rounded(proj[j, rows - 8 :, :])
        rim_copy = pltpu.make_async_remote_copy(
            src_ref=rim_out.at[h],
            dst_ref=rim_in.at[h],
            send_sem=rim_send_sem.at[h],
            recv_sem=rim_recv_sem.at[h],
            device_id={"seq": lax.rem(place + 1, seq_size)},
            device_id_type=MESH,
        )
        rim_copy.start()
        rim_copy.wait()

        def first_pass(g, carry):
            lanes = pl.ds(pl.multiple_of(g * LANES, LANES), LANES)
            feat = []
            for j in range(FEAT):
                now = rounded(proj[j, :, lanes])
                before = 0.0 if h == 0 else rim_in[0, j, :, lanes]
                padded[j, 8:, :] = now
                padded[j, :8, :] = jnp.where(place > 0, rim_in[h, j, :, lanes], before)
                total = filter_ref[0, j : j + 1, lanes] * now
                for offset in range(1, FEAT):
                    total = (
                        total
                        + filter_ref[offset, j : j + 1, lanes]
                        * padded[j, pl.ds(8 - offset, rows), :]
                    )
                feat.append(rounded(total))
            query_buf[g] = feat[0]
            driven_buf[g] = feat[1] * feat[2]
            decay = decay_ref[:, lanes]
            lam = spread(jnp.exp(-decay))

            def step(i, state):
                x = driven_buf[g, pl.ds(i, SEGS, stride=seg), :]
                return lam * state + x[None]

            state = lax.fori_loop(
                0, seg, step, jnp.zeros((modes, SEGS, LANES), jnp.float32), unroll=8
            )
            seg_ends[g] = state
            lam_seg = jnp.exp(-decay * seg)
            end = state[:, 0, :]
            for s in range(1, SEGS):
                end = lam_seg * end + state[:, s, :]
            own_end[:, lanes] = end
            return carry

        def end_copy(half, to, source):
            cols = pl.ds(half * width, width)
            return pltpu.make_async_remote_copy(
                src_ref=own_end.at[:, cols],
                dst_ref=all_ends.at[h, source, :, cols],
                send_sem=end_send_sem.at[h, half, to],
                recv_sem=end_recv_sem.at[h, half, source],
                device_id={"seq": to},
                device_id_type=MESH,
            )

        for half in range(halves):
            lax.fori_loop(half * per_half, (half + 1) * per_half, first_pass, 0)
            for k in range(1, seq_size):
                end_copy(half, lax.rem(place + k, seq_size), place).start()
        all_ends[h, place] = own_end[...]

        def second_pass(g, carry):
            lanes = pl.ds(pl.multiple_of(g * LANES, LANES), LANES)
            decay = decay_ref[:, lanes]
            lam_seg = jnp.exp(-decay * seg)
            start = incoming[:, lanes]
            for s in range(SEGS):
                seg_starts[:, s, :] = start
                start = lam_seg * start + seg_ends[g, :, s, :]
            lam = spread(jnp.exp(-decay))
            gain = spread(residue_ref[:, lanes])
            skip = jnp.broadcast_to(skip_ref[:, lanes], (SEGS, LANES))

            def step(i, state):
                at = pl.ds(i, SEGS, stride=seg)
                x = driven_buf[g, at, :]
                state = lam * state + x[None]
                long = jnp.sum(gain * state, axis=0) + skip * x
                hidden_f[at, :] = query_buf[g, at, :] * long
                return state

            lax.fori_loop(0, seg, step, seg_starts[...], unroll=8)
            hidden[h, :, lanes] = hidden_f[...].astype(jnp.bfloat16)
            return carry

        for half in range(halves):
            for k in range(1, seq_size):
                peer = lax.rem(place + k, seq_size)
                end_copy(half, peer, place).wait_send()
                end_copy(half, peer, peer).wait_recv()
            cols = slice(half * width, (half + 1) * width)
            span = jnp.exp(-decay_ref[:, cols] * rows)
            state = jnp.zeros((modes, width), jnp.float32)
            if h == 1:
                for p in range(seq_size):
                    state = span * state + all_ends[0, p, :, cols]
            for p in range(seq_size - 1):
                state = jnp.where(p < place, span * state + all_ends[h, p, :, cols], state)
            incoming[:, cols] = state
            lax.fori_loop(half * per_half, (half + 1) * per_half, second_pass, 0)

    def project(h, dest):
        def one(t, carry):
            cols = pl.ds(pl.multiple_of(t * tile, tile), tile)
            part[:, cols] = jnp.dot(
                hidden[h], weight_buf[dest, :, cols], preferred_element_type=jnp.float32
            )
            return carry

        lax.fori_loop(0, tiles, one, 0)

    def sum_copy(h, way, dest, to):
        return pltpu.make_async_remote_copy(
            src_ref=sums_out.at[h, way, dest],
            dst_ref=sums_in.at[h, way, dest],
            send_sem=sum_send_sem.at[h, way, dest],
            recv_sem=sum_recv_sem.at[h, way, dest],
            device_id={"chan": to},
            device_id_type=MESH,
        )

    def begin_sums(h):
        def begin(way, dest, to):
            project(h, dest)
            sums_out[h, way, dest] = part[...].astype(jnp.bfloat16)
            sum_copy(h, way, dest, to).start()

        def one(i, carry):
            pl.when(shard == 0)(functools.partial(begin, 0, last - i, shard + 1))
            pl.when(shard == last)(functools.partial(begin, 1, i, shard - 1))
            return carry

        lax.fori_loop(0, last, one, 0)

    def add_sums(h):
        def pass_on(way, dest, to):
            project(h, dest)
            sum_copy(h, way, dest, to).wait_recv()
            sums_out[h, way, dest] = (
                part[...] + sums_in[h, way, dest].astype(jnp.float32)
            ).astype(jnp.bfloat16)
            sum_copy(h, way, dest, to).start()

        def sum_step(t, carry):
            up = last - (t - shard)
            pl.when(inner & (t >= shard) & (up > shard))(
                functools.partial(pass_on, 0, up, shard + 1)
            )
            down = t - (last - shard)
            pl.when(inner & (down >= 0) & (down < shard))(
                functools.partial(pass_on, 1, down, shard - 1)
            )
            return carry

        lax.fori_loop(0, 2 * last, sum_step, 0)

    def result_copy(h, half, to):
        return pltpu.make_async_remote_copy(
            src_ref=result_out.at[h],
            dst_ref=result_in.at[half],
            send_sem=result_send_sem.at[h],
            recv_sem=result_recv_sem.at[half],
            device_id={"seq": to},
            device_id_type=MESH,
        )

    def finish(h):
        project(h, shard)
        part[...] += gathered[h, shard].astype(jnp.float32)

        @pl.when(shard > 0)
        def _():
            sum_copy(h, 0, shard, 0).wait_recv()
            part[...] += sums_in[h, 0, shard].astype(jnp.float32)

        @pl.when(shard < last)
        def _():
            sum_copy(h, 1, shard, 0).wait_recv()
            part[...] += sums_in[h, 1, shard].astype(jnp.float32)

        block = h * seq_size + place
        to, half = block // 2, lax.rem(block, 2)
        result_out[h] = part[...].astype(jnp.bfloat16)

        @pl.when(to != place)
        def _():
            result_copy(h, half, to).start()

        @pl.when(to == place)
        def _():
            result_in[half] = result_out[h]

    gather(0)
    pl.when(inner)(functools.partial(send_own, 1))
    middle(0)
    for copy in weight_copies:
        copy.wait()
    begin_sums(0)
    gather(1)
    middle(1)
    begin_sums(1)
    add_sums(0)
    finish(0)
    add_sums(1)
    finish(1)

    for h in range(2):
        block = h * seq_size + place

        @pl.when(block // 2 != place)
        def _():
            result_copy(h, 0, 0).wait_send()

        def drain(dest, carry):
            @pl.when(dest > shard)
            def _():
                sum_copy(h, 0, dest, 0).wait_send()

            @pl.when(dest < shard)
            def _():
                sum_copy(h, 1, dest, 0).wait_send()

            @pl.when((dest <= shard) & (shard < last))
            def _():
                gather_copy(h, 0, dest, 0).wait_send()

            @pl.when((dest >= shard) & (shard > 0))
            def _():
                gather_copy(h, 1, dest, 0).wait_send()

            return carry

        lax.fori_loop(0, chan_size, drain, 0)

    for half in range(2):
        block = 2 * place + half

        @pl.when(lax.rem(block, seq_size) != place)
        def _():
            token_copy(half, 0, 0).wait_send()
            result_copy(0, half, 0).wait_recv()

        out_ref[half * rows : (half + 1) * rows, :] = result_in[half]


def on_device(
    seq_size,
    chan_size,
    tokens,
    embedding,
    norm_gain,
    in_weight,
    short_filter,
    decay_rate,
    residue,
    skip_gain,
    out_weight,
):
    rows = tokens.shape[0] // 2
    channels = embedding.shape[1]
    modes = decay_rate.shape[0]
    groups = channels // LANES
    f32, bf16 = jnp.float32, jnp.bfloat16
    vmem = pl.BlockSpec(memory_space=pltpu.VMEM)
    hbm = pl.BlockSpec(memory_space=pl.ANY)
    dma = pltpu.SemaphoreType.DMA
    return pl.pallas_call(
        functools.partial(block_kernel, seq_size, chan_size),
        out_shape=jax.ShapeDtypeStruct((2 * rows, channels), bf16),
        in_specs=[vmem] * 7 + [hbm] * 2,
        out_specs=vmem,
        scratch_shapes=[
            pltpu.VMEM((chan_size, FEAT, channels, channels), bf16),
            pltpu.VMEM((chan_size, channels, channels), bf16),
            pltpu.VMEM((2, 1, rows), jnp.int32),
            pltpu.VMEM((2, chan_size, rows, channels), bf16),
            pltpu.VMEM((2, 8, rows), f32),
            pltpu.VMEM((2, chan_size, 8, rows), f32),
            pltpu.VMEM((rows, channels), bf16),
            pltpu.VMEM((FEAT, rows, channels), f32),
            pltpu.VMEM((2, FEAT, 8, channels), f32),
            pltpu.VMEM((2, FEAT, 8, channels), f32),
            pltpu.VMEM((FEAT, rows + 8, LANES), f32),
            pltpu.VMEM((groups, rows, LANES), f32),
            pltpu.VMEM((groups, rows, LANES), f32),
            pltpu.VMEM((groups, modes, SEGS, LANES), f32),
            pltpu.VMEM((modes, channels), f32),
            pltpu.VMEM((2, seq_size, modes, channels), f32),
            pltpu.VMEM((modes, channels), f32),
            pltpu.VMEM((modes, SEGS, LANES), f32),
            pltpu.VMEM((rows, LANES), f32),
            pltpu.VMEM((2, rows, channels), bf16),
            pltpu.VMEM((rows, channels), f32),
            pltpu.VMEM((2, 2, chan_size, rows, channels), bf16),
            pltpu.VMEM((2, 2, chan_size, rows, channels), bf16),
            pltpu.VMEM((2, rows, channels), bf16),
            pltpu.VMEM((2, rows, channels), bf16),
            dma((chan_size, FEAT)),
            dma((chan_size,)),
            dma((2,)),
            dma((2,)),
            dma((2, chan_size)),
            dma((2, chan_size)),
            dma((2, 2, chan_size)),
            dma((2, chan_size)),
            dma((2,)),
            dma((2,)),
            dma((2, 2, seq_size)),
            dma((2, 2, seq_size)),
            dma((2, 2, chan_size)),
            dma((2, 2, chan_size)),
            dma((2,)),
            dma((2,)),
        ],
        compiler_params=pltpu.CompilerParams(
            collective_id=0, has_side_effects=True, vmem_limit_bytes=60 << 20
        ),
    )(
        tokens.reshape(2, 1, rows),
        embedding,
        norm_gain.reshape(1, -1),
        short_filter,
        decay_rate,
        residue,
        skip_gain.reshape(1, channels),
        in_weight.transpose(1, 0, 2),
        out_weight,
    )


def solution(mesh):
    placed = (
        P("seq"),
        P(None, "chan"),
        P(),
        P(None, None, "chan"),
        P(None, None, "chan"),
        P(None, "chan"),
        P(None, "chan"),
        P("chan"),
        P("chan", None),
    )
    return jax.shard_map(
        functools.partial(on_device, mesh.shape["seq"], mesh.shape["chan"]),
        mesh=mesh,
        in_specs=placed,
        out_specs=P("seq", "chan"),
        check_vma=False,
    )
```

time: 106 us -> 116 us (1.094)
  Pallas kernels: 104 us -> 114 us
    pallas_call x1, Pallas kernels: 104 us -> 114 us  [on_device(): pl.pallas_call(functools.partial(block_kernel, seq_size, chan_size), out_...]
where the time goes in v3:
time: 116 us; the launch traced here: 115 us
  Pallas kernels  114 us (98%)
  local copies, waits for them, and re-layouts  1.87 us (2%)
    pallas_call x1, Pallas kernels, on_device(): pl.pallas_call(functools.partial(block_kernel, seq_size, chan_size), out_...  114 us

profile of v3, /device:TPU:0, one launch (start us, length us, event | category | flops | bytes accessed | tf_op | source)
XLA Modules:
  0.0 115.4 jit_solution(15158094281775530468)
XLA Ops:
  0.0 113.6 %shard_map.91 = bf16[256,1024]{1,0:T(8,128)(2,1)} custom-call(s32[2,1,128]{2,1,0:T(1,128)} %bitcast.7, bf16[512,1024]{1,0:T(8,128)(2,1)} %embed_ref.1, f32[1,4096]{1,0:T(1,128)} %bitcast.5, f32[3,3,1024]{2,1,0:T(4,128)} %filter_ref.1, f32[16,1024]{1,0:T(8,128)} %decay_ref.1, f32[16,1024]{1,0:T(8,128)} %residue_ref.1, f32[1,1024]{1,0:T(1,128)} %bitcast.6, ...), custom_call_target="tpu_custom_call" | custom-call | tf_op jit(solution)/shard_map/pallas_call | solution.py:547
  113.6 1.9 %copy.11 = bf16[256,1024]{1,0:T(8,128)(2,1)} copy(bf16[256,1024]{1,0:T(8,128)(2,1)} %shard_map.91) | data formatting | bytes 1048576

commit v4 on v3

--- a/solution.py
+++ b/solution.py
@@ -43,7 +43,7 @@
     own_end,
     all_ends,
     incoming,
-    seg_starts,
+    factors,
     hidden_f,
     hidden,
     part,
@@ -199,10 +199,26 @@
 
     first = look_up(0)
     send_own(0)
-    send_squares(0, first)
     second = look_up(1)
     pl.when(outer)(functools.partial(send_own, 1))
+    send_squares(0, first)
     send_squares(1, second)
+
+    def spread(value):
+        return jnp.broadcast_to(value[:, None, :], (value.shape[0], SEGS, LANES))
+
+    def make_factors(g, carry):
+        lanes = pl.ds(pl.multiple_of(g * LANES, LANES), LANES)
+        decay = spread(decay_ref[:, lanes])
+        left = (SEGS - 1 - lax.broadcasted_iota(jnp.int32, (1, SEGS, LANES), 1)) * seg
+        factors[0, g] = jnp.exp(-decay)
+        factors[1, g] = spread(residue_ref[:, lanes])
+        factors[2, g] = jnp.exp(-decay * seg)
+        factors[3, g] = jnp.exp(-decay * left.astype(jnp.float32))
+        return carry
+
+    lax.fori_loop(0, groups, make_factors, 0)
+    proj[...] = jnp.zeros_like(proj)
 
     def row_scale(h):
         total = squares_out[h]
@@ -213,33 +229,34 @@
             total = total + squares_in[h, peer]
         return lax.rsqrt(total.T[:, :1] * (1.0 / (channels * chan_size)) + 1e-06)
 
+    scales = [row_scale(0), row_scale(1)]
+
+    def absorb(h, which):
+        cols = pl.ds(pl.multiple_of(which * channels, channels), channels)
+        normed[...] = (
+            gathered[h, which].astype(jnp.float32) * scales[h] * norm_ref[:, cols]
+        ).astype(jnp.bfloat16)
+
+        def one(t, carry):
+            j = t // tiles
+            at = pl.ds(pl.multiple_of((t % tiles) * tile, tile), tile)
+            proj[h, j, :, at] += jnp.dot(
+                normed[...], in_buf[which, j, :, at], preferred_element_type=jnp.float32
+            )
+            return carry
+
+        lax.fori_loop(0, FEAT * tiles, one, 0)
+
     def gather(h):
-        proj[...] = jnp.zeros_like(proj)
-        scale = row_scale(h)
-
-        def absorb(which):
+        def take(which):
             if h == 0:
                 for j in range(FEAT):
                     in_copy(which, j).wait()
-            cols = pl.ds(pl.multiple_of(which * channels, channels), channels)
-            normed[...] = (
-                gathered[h, which].astype(jnp.float32) * scale * norm_ref[:, cols]
-            ).astype(jnp.bfloat16)
-
-            def one(t, carry):
-                j = t // tiles
-                at = pl.ds(pl.multiple_of((t % tiles) * tile, tile), tile)
-                proj[j, :, at] += jnp.dot(
-                    normed[...], in_buf[which, j, :, at], preferred_element_type=jnp.float32
-                )
-                return carry
-
-            lax.fori_loop(0, FEAT * tiles, one, 0)
+            absorb(h, which)
 
         if h == 0:
-            absorb(shard)
-        else:
-            pl.when(outer)(functools.partial(absorb, shard))
+            take(shard)
+            absorb(1, shard)
 
         def gather_step(k, carry):
             below, above = shard - k, shard + k
@@ -254,19 +271,19 @@
                 gather_copy(h, 1, above, 0).wait_recv()
                 send_down(h, above)
 
-            pl.when(below >= 0)(functools.partial(absorb, below))
-            pl.when(above <= last)(functools.partial(absorb, above))
+            pl.when(below >= 0)(functools.partial(take, below))
+            pl.when(above <= last)(functools.partial(take, above))
             return carry
 
         lax.fori_loop(1, chan_size, gather_step, 0)
-        if h == 1:
-            pl.when(inner)(functools.partial(absorb, shard))
 
     def rounded(value):
         return value.astype(jnp.bfloat16).astype(jnp.float32)
 
-    def spread(value):
-        return jnp.broadcast_to(value[:, None, :], (value.shape[0], SEGS, LANES))
+    sublane = lax.broadcasted_iota(jnp.int32, (1, SEGS, LANES), 1)
+
+    def shifted(value, by):
+        return pltpu.roll(value, by, axis=1)
 
     halves = 2 if groups > 1 else 1
     width = channels // halves
@@ -274,7 +291,7 @@
 
     def middle(h):
         for j in range(FEAT):
-            rim_out[h, j] = rounded(proj[j, rows - 8 :, :])
+            rim_out[h, j] = rounded(proj[h, j, rows - 8 :, :])
         rim_copy = pltpu.make_async_remote_copy(
             src_ref=rim_out.at[h],
             dst_ref=rim_in.at[h],
@@ -284,28 +301,37 @@
             device_id_type=MESH,
         )
         rim_copy.start()
-        rim_copy.wait()
-
-        def first_pass(g, carry):
+
+        def featurize(g, count, with_rim):
             lanes = pl.ds(pl.multiple_of(g * LANES, LANES), LANES)
             feat = []
             for j in range(FEAT):
-                now = rounded(proj[j, :, lanes])
-                before = 0.0 if h == 0 else rim_in[0, j, :, lanes]
-                padded[j, 8:, :] = now
-                padded[j, :8, :] = jnp.where(place > 0, rim_in[h, j, :, lanes], before)
+                now = rounded(proj[h, j, :count, lanes])
+                padded[j, 8 : 8 + count, :] = now
+                if with_rim:
+                    before = 0.0 if h == 0 else rim_in[0, j, :, lanes]
+                    padded[j, :8, :] = jnp.where(place > 0, rim_in[h, j, :, lanes], before)
+                else:
+                    padded[j, :8, :] = jnp.zeros((8, LANES), jnp.float32)
                 total = filter_ref[0, j : j + 1, lanes] * now
                 for offset in range(1, FEAT):
                     total = (
                         total
                         + filter_ref[offset, j : j + 1, lanes]
-                        * padded[j, pl.ds(8 - offset, rows), :]
+                        * padded[j, pl.ds(8 - offset, count), :]
                     )
                 feat.append(rounded(total))
-            query_buf[g] = feat[0]
-            driven_buf[g] = feat[1] * feat[2]
-            decay = decay_ref[:, lanes]
-            lam = spread(jnp.exp(-decay))
+            query_buf[g, :count, :] = feat[0]
+            driven_buf[g, :count, :] = feat[1] * feat[2]
+
+        def feature_pass(g, carry):
+            featurize(g, rows, False)
+            return carry
+
+        def first_pass(g, carry):
+            lanes = pl.ds(pl.multiple_of(g * LANES, LANES), LANES)
+            featurize(g, 16, True)
+            lam = factors[0, g]
 
             def step(i, state):
                 x = driven_buf[g, pl.ds(i, SEGS, stride=seg), :]
@@ -315,11 +341,14 @@
                 0, seg, step, jnp.zeros((modes, SEGS, LANES), jnp.float32), unroll=8
             )
             seg_ends[g] = state
-            lam_seg = jnp.exp(-decay * seg)
-            end = state[:, 0, :]
-            for s in range(1, SEGS):
-                end = lam_seg * end + state[:, s, :]
-            own_end[:, lanes] = end
+            end = factors[3, g] * state
+            for by in (4, 2, 1):
+                end = end + shifted(end, by)
+            end = end.reshape(modes // SEGS, SEGS, SEGS, LANES)
+            mode = lax.broadcasted_iota(jnp.int32, (1, SEGS, SEGS, LANES), 1)
+            row = lax.broadcasted_iota(jnp.int32, (1, SEGS, SEGS, LANES), 2)
+            end = jnp.sum(jnp.where(mode == row, end, 0.0), axis=1)
+            own_end[:, lanes] = end.reshape(modes, LANES)
             return carry
 
         def end_copy(half, to, source):
@@ -334,6 +363,9 @@
             )
 
         for half in range(halves):
+            lax.fori_loop(half * per_half, (half + 1) * per_half, feature_pass, 0)
+            if half == 0:
+                rim_copy.wait()
             lax.fori_loop(half * per_half, (half + 1) * per_half, first_pass, 0)
             for k in range(1, seq_size):
                 end_copy(half, lax.rem(place + k, seq_size), place).start()
@@ -341,14 +373,13 @@
 
         def second_pass(g, carry):
             lanes = pl.ds(pl.multiple_of(g * LANES, LANES), LANES)
-            decay = decay_ref[:, lanes]
-            lam_seg = jnp.exp(-decay * seg)
-            start = incoming[:, lanes]
-            for s in range(SEGS):
-                seg_starts[:, s, :] = start
-                start = lam_seg * start + seg_ends[g, :, s, :]
-            lam = spread(jnp.exp(-decay))
-            gain = spread(residue_ref[:, lanes])
+            start = jnp.where(sublane > 0, shifted(seg_ends[g], 1), spread(incoming[:, lanes]))
+            power = factors[2, g]
+            for by in (1, 2, 4):
+                start = start + jnp.where(sublane >= by, power * shifted(start, by), 0.0)
+                power = power * power
+            lam = factors[0, g]
+            gain = factors[1, g]
             skip = jnp.broadcast_to(skip_ref[:, lanes], (SEGS, LANES))
 
             def step(i, state):
@@ -359,7 +390,7 @@
                 hidden_f[at, :] = query_buf[g, at, :] * long
                 return state
 
-            lax.fori_loop(0, seg, step, seg_starts[...], unroll=8)
+            lax.fori_loop(0, seg, step, start, unroll=8)
             hidden[h, :, lanes] = hidden_f[...].astype(jnp.bfloat16)
             return carry
 
@@ -557,7 +588,7 @@
             pltpu.VMEM((2, 8, rows), f32),
             pltpu.VMEM((2, chan_size, 8, rows), f32),
             pltpu.VMEM((rows, channels), bf16),
-            pltpu.VMEM((FEAT, rows, channels), f32),
+            pltpu.VMEM((2, FEAT, rows, channels), f32),
             pltpu.VMEM((2, FEAT, 8, channels), f32),
             pltpu.VMEM((2, FEAT, 8, channels), f32),
             pltpu.VMEM((FEAT, rows + 8, LANES), f32),
@@ -567,7 +598,7 @@
             pltpu.VMEM((modes, channels), f32),
             pltpu.VMEM((2, seq_size, modes, channels), f32),
             pltpu.VMEM((modes, channels), f32),
-            pltpu.VMEM((modes, SEGS, LANES), f32),
+            pltpu.VMEM((4, groups, modes, SEGS, LANES), f32),
             pltpu.VMEM((rows, LANES), f32),
             pltpu.VMEM((2, rows, channels), bf16),
             pltpu.VMEM((rows, channels), f32),

time: 116 us -> 119 us (1.026)
  Pallas kernels: 114 us -> 117 us
    pallas_call x1, Pallas kernels: 114 us -> 117 us  [on_device(): pl.pallas_call(functools.partial(block_kernel, seq_size, chan_size), out_...]
where the time goes in v4:
time: 119 us
  Pallas kernels  117 us (98%)
  local copies, waits for them, and re-layouts  1.87 us (2%)
    pallas_call x1, Pallas kernels, on_device(): pl.pallas_call(functools.partial(block_kernel, seq_size, chan_size), out_...  117 us

profile of v4, /device:TPU:0, one launch (start us, length us, event | category | flops | bytes accessed | tf_op | source)
XLA Modules:
  0.0 119.3 jit_solution(6280060996239177842)
XLA Ops:
  0.0 117.4 %shard_map.91 = bf16[256,1024]{1,0:T(8,128)(2,1)} custom-call(s32[2,1,128]{2,1,0:T(1,128)} %bitcast.7, bf16[512,1024]{1,0:T(8,128)(2,1)} %embed_ref.1, f32[1,4096]{1,0:T(1,128)} %bitcast.5, f32[3,3,1024]{2,1,0:T(4,128)} %filter_ref.1, f32[16,1024]{1,0:T(8,128)} %decay_ref.1, f32[16,1024]{1,0:T(8,128)} %residue_ref.1, f32[1,1024]{1,0:T(1,128)} %bitcast.6, ...), custom_call_target="tpu_custom_call" | custom-call | tf_op jit(solution)/shard_map/pallas_call | solution.py:578
  117.4 1.9 %copy.11 = bf16[256,1024]{1,0:T(8,128)(2,1)} copy(bf16[256,1024]{1,0:T(8,128)(2,1)} %shard_map.91) | data formatting | bytes 1048576

commit v5 on v2

--- a/solution.py
+++ b/solution.py
@@ -42,7 +42,7 @@
     own_end,
     all_ends,
     incoming,
-    seg_starts,
+    factors,
     hidden_f,
     hidden,
     part,
@@ -81,6 +81,15 @@
         for j in range(FEAT):
             in_copy(d, j).start()
 
+    barrier = pltpu.get_barrier_semaphore()
+    for k in range(1, seq_size):
+        pl.semaphore_signal(
+            barrier, 1, device_id={"seq": lax.rem(place + k, seq_size)}, device_id_type=MESH
+        )
+    for k in range(1, chan_size):
+        pl.semaphore_signal(
+            barrier, 1, device_id={"chan": lax.rem(shard + k, chan_size)}, device_id_type=MESH
+        )
     start_in(shard)
     for k in range(1, chan_size):
         pl.when(shard - k >= 0)(functools.partial(start_in, shard - k))
@@ -94,21 +103,46 @@
     for copy in weight_copies:
         copy.start()
 
-    barrier = pltpu.get_barrier_semaphore()
-    for k in range(1, seq_size):
-        pl.semaphore_signal(
-            barrier, 1, device_id={"seq": lax.rem(place + k, seq_size)}, device_id_type=MESH
-        )
-    for k in range(1, chan_size):
-        pl.semaphore_signal(
-            barrier, 1, device_id={"chan": lax.rem(shard + k, chan_size)}, device_id_type=MESH
-        )
     ids = lax.broadcasted_iota(jnp.int32, (vocab, rows), 0)
     one_hot = (ids == tokens_ref[...]).astype(jnp.float32).astype(jnp.bfloat16)
     stream = lax.dot_general(
         one_hot, embed_ref[...], (((0,), (0,)), ((), ())), preferred_element_type=jnp.float32
     )
     gathered[shard] = stream.astype(jnp.bfloat16)
+    pl.semaphore_wait(barrier, seq_size - 1 + chan_size - 1)
+
+    def square_copy(to, source):
+        return pltpu.make_async_remote_copy(
+            src_ref=squares_out,
+            dst_ref=squares_in.at[source],
+            send_sem=square_send_sem.at[to],
+            recv_sem=square_recv_sem.at[source],
+            device_id={"chan": to},
+            device_id_type=MESH,
+        )
+
+    def gather_copy(way, which, to):
+        return pltpu.make_async_remote_copy(
+            src_ref=gathered.at[which],
+            dst_ref=gathered.at[which],
+            send_sem=gather_send_sem.at[way, which],
+            recv_sem=gather_recv_sem.at[which],
+            device_id={"chan": to},
+            device_id_type=MESH,
+        )
+
+    def send_up(which):
+        @pl.when(shard < last)
+        def _():
+            gather_copy(0, which, shard + 1).start()
+
+    def send_down(which):
+        @pl.when(shard > 0)
+        def _():
+            gather_copy(1, which, shard - 1).start()
+
+    send_up(shard)
+    send_down(shard)
     ones = jnp.ones((8, channels), jnp.float32)
     squares_out[...] = lax.dot_general(
         ones,
@@ -117,43 +151,8 @@
         precision=lax.Precision.HIGHEST,
         preferred_element_type=jnp.float32,
     )
-    pl.semaphore_wait(barrier, seq_size - 1 + chan_size - 1)
-
-    def square_copy(to, source):
-        return pltpu.make_async_remote_copy(
-            src_ref=squares_out,
-            dst_ref=squares_in.at[source],
-            send_sem=square_send_sem.at[to],
-            recv_sem=square_recv_sem.at[source],
-            device_id={"chan": to},
-            device_id_type=MESH,
-        )
-
-    def gather_copy(way, which, to):
-        return pltpu.make_async_remote_copy(
-            src_ref=gathered.at[which],
-            dst_ref=gathered.at[which],
-            send_sem=gather_send_sem.at[way, which],
-            recv_sem=gather_recv_sem.at[which],
-            device_id={"chan": to},
-            device_id_type=MESH,
-        )
-
     for k in range(1, chan_size):
         square_copy(lax.rem(shard + k, chan_size), shard).start()
-
-    def send_up(which):
-        @pl.when(shard < last)
-        def _():
-            gather_copy(0, which, shard + 1).start()
-
-    def send_down(which):
-        @pl.when(shard > 0)
-        def _():
-            gather_copy(1, which, shard - 1).start()
-
-    send_up(shard)
-    send_down(shard)
     proj[...] = jnp.zeros_like(proj)
     total = squares_out[...]
     for k in range(1, chan_size):
@@ -183,6 +182,19 @@
 
     absorb(shard)
 
+    def spread(value):
+        return jnp.broadcast_to(value[:, None, :], (value.shape[0], SEGS, LANES))
+
+    def make_factors(g, carry):
+        lanes = pl.ds(pl.multiple_of(g * LANES, LANES), LANES)
+        decay = spread(decay_ref[:, lanes])
+        left = (SEGS - 1 - lax.broadcasted_iota(jnp.int32, (1, SEGS, LANES), 1)) * seg
+        factors[0, g] = jnp.exp(-decay)
+        factors[1, g] = spread(residue_ref[:, lanes])
+        factors[2, g] = jnp.exp(-decay * seg)
+        factors[3, g] = jnp.exp(-decay * left.astype(jnp.float32))
+        return carry
+
     def gather_step(k, carry):
         below, above = shard - k, shard + k
 
@@ -198,6 +210,11 @@
 
         pl.when(below >= 0)(functools.partial(absorb, below))
         pl.when(above <= last)(functools.partial(absorb, above))
+
+        @pl.when(k == 1)
+        def _():
+            lax.fori_loop(0, groups, make_factors, 0)
+
         return carry
 
     lax.fori_loop(1, chan_size, gather_step, 0)
@@ -216,30 +233,40 @@
         device_id_type=MESH,
     )
     rim_copy.start()
-    rim_copy.wait()
     keep = (place > 0).astype(jnp.float32)
-
-    def spread(value):
-        return jnp.broadcast_to(value[:, None, :], (value.shape[0], SEGS, LANES))
-
-    def first_pass(g, carry):
+    sublane = lax.broadcasted_iota(jnp.int32, (1, SEGS, LANES), 1)
+
+    def shifted(value, by):
+        return pltpu.roll(value, by, axis=1)
+
+    def featurize(g, count, with_rim):
         lanes = pl.ds(pl.multiple_of(g * LANES, LANES), LANES)
         feat = []
         for j in range(FEAT):
-            now = rounded(proj[j, :, lanes])
-            padded[j, 8:, :] = now
-            padded[j, :8, :] = rim_in[j, :, lanes] * keep
+            now = rounded(proj[j, :count, lanes])
+            padded[j, 8 : 8 + count, :] = now
+            if with_rim:
+                padded[j, :8, :] = rim_in[j, :, lanes] * keep
+            else:
+                padded[j, :8, :] = jnp.zeros((8, LANES), jnp.float32)
             total = filter_ref[0, j : j + 1, lanes] * now
             for offset in range(1, FEAT):
                 total = (
                     total
-                    + filter_ref[offset, j : j + 1, lanes] * padded[j, pl.ds(8 - offset, rows), :]
+                    + filter_ref[offset, j : j + 1, lanes] * padded[j, pl.ds(8 - offset, count), :]
                 )
             feat.append(rounded(total))
-        query_buf[g] = feat[0]
-        driven_buf[g] = feat[1] * feat[2]
-        decay = decay_ref[:, lanes]
-        lam = spread(jnp.exp(-decay))
+        query_buf[g, :count, :] = feat[0]
+        driven_buf[g, :count, :] = feat[1] * feat[2]
+
+    def feature_pass(g, carry):
+        featurize(g, rows, False)
+        return carry
+
+    def first_pass(g, carry):
+        lanes = pl.ds(pl.multiple_of(g * LANES, LANES), LANES)
+        featurize(g, 16, True)
+        lam = factors[0, g]
 
         def step(i, state):
             x = driven_buf[g, pl.ds(i, SEGS, stride=seg), :]
@@ -249,11 +276,14 @@
             0, seg, step, jnp.zeros((modes, SEGS, LANES), jnp.float32), unroll=8
         )
         seg_ends[g] = state
-        lam_seg = jnp.exp(-decay * seg)
-        end = state[:, 0, :]
-        for s in range(1, SEGS):
-            end = lam_seg * end + state[:, s, :]
-        own_end[:, lanes] = end
+        end = factors[3, g] * state
+        for by in (4, 2, 1):
+            end = end + shifted(end, by)
+        end = end.reshape(modes // SEGS, SEGS, SEGS, LANES)
+        mode = lax.broadcasted_iota(jnp.int32, (1, SEGS, SEGS, LANES), 1)
+        row = lax.broadcasted_iota(jnp.int32, (1, SEGS, SEGS, LANES), 2)
+        end = jnp.sum(jnp.where(mode == row, end, 0.0), axis=1)
+        own_end[:, lanes] = end.reshape(modes, LANES)
         return carry
 
     halves = 2 if groups > 1 else 1
@@ -272,6 +302,9 @@
         )
 
     for half in range(halves):
+        lax.fori_loop(half * per_half, (half + 1) * per_half, feature_pass, 0)
+        if half == 0:
+            rim_copy.wait()
         lax.fori_loop(half * per_half, (half + 1) * per_half, first_pass, 0)
         for k in range(1, seq_size):
             end_copy(half, lax.rem(place + k, seq_size), place).start()
@@ -279,14 +312,13 @@
 
     def second_pass(g, carry):
         lanes = pl.ds(pl.multiple_of(g * LANES, LANES), LANES)
-        decay = decay_ref[:, lanes]
-        lam_seg = jnp.exp(-decay * seg)
-        start = incoming[:, lanes]
-        for s in range(SEGS):
-            seg_starts[:, s, :] = start
-            start = lam_seg * start + seg_ends[g, :, s, :]
-        lam = spread(jnp.exp(-decay))
-        gain = spread(residue_ref[:, lanes])
+        start = jnp.where(sublane > 0, shifted(seg_ends[g], 1), spread(incoming[:, lanes]))
+        power = factors[2, g]
+        for by in (1, 2, 4):
+            start = start + jnp.where(sublane >= by, power * shifted(start, by), 0.0)
+            power = power * power
+        lam = factors[0, g]
+        gain = factors[1, g]
         skip = jnp.broadcast_to(skip_ref[:, lanes], (SEGS, LANES))
 
         def step(i, state):
@@ -297,7 +329,7 @@
             hidden_f[at, :] = query_buf[g, at, :] * long
             return state
 
-        lax.fori_loop(0, seg, step, seg_starts[...], unroll=8)
+        lax.fori_loop(0, seg, step, start, unroll=8)
         hidden[:, lanes] = hidden_f[...].astype(jnp.bfloat16)
         return carry
 
@@ -449,7 +481,7 @@
             pltpu.VMEM((modes, channels), f32),
             pltpu.VMEM((seq_size, modes, channels), f32),
             pltpu.VMEM((modes, channels), f32),
-            pltpu.VMEM((modes, SEGS, LANES), f32),
+            pltpu.VMEM((4, groups, modes, SEGS, LANES), f32),
             pltpu.VMEM((rows, LANES), f32),
             pltpu.VMEM((rows, channels), bf16),
             pltpu.VMEM((rows, channels), f32),

time: 106 us -> 110 us (1.038)
  Pallas kernels: 104 us -> 108 us
    pallas_call x1, Pallas kernels: 104 us -> 108 us  [on_device(): pl.pallas_call(functools.partial(block_kernel, seq_size, chan_size), out_...]
where the time goes in v5:
time: 110 us
  Pallas kernels  108 us (98%)
  local copies, waits for them, and re-layouts  1.87 us (2%)
    pallas_call x1, Pallas kernels, on_device(): pl.pallas_call(functools.partial(block_kernel, seq_size, chan_size), out_...  108 us

profile of v5, /device:TPU:0, one launch (start us, length us, event | category | flops | bytes accessed | tf_op | source)
XLA Modules:
  0.0 110.3 jit_solution(13558904329070948035)
XLA Ops:
  0.0 108.4 %shard_map.91 = bf16[256,1024]{1,0:T(8,128)(2,1)} custom-call(s32[1,256]{1,0:T(1,128)} %bitcast.7, bf16[512,1024]{1,0:T(8,128)(2,1)} %embed_ref.1, f32[1,4096]{1,0:T(1,128)} %bitcast.5, f32[3,3,1024]{2,1,0:T(4,128)} %filter_ref.1, f32[16,1024]{1,0:T(8,128)} %decay_ref.1, f32[16,1024]{1,0:T(8,128)} %residue_ref.1, f32[1,1024]{1,0:T(1,128)} %bitcast.6, ...), custom_call_target="tpu_custom_call" | custom-call | tf_op jit(solution)/shard_map/pallas_call | solution.py:462
  108.4 1.9 %copy.11 = bf16[256,1024]{1,0:T(8,128)(2,1)} copy(bf16[256,1024]{1,0:T(8,128)(2,1)} %shard_map.91) | data formatting | bytes 1048576

commit v6 on v5

--- a/solution.py
+++ b/solution.py
@@ -46,7 +46,6 @@
     hidden_f,
     hidden,
     part,
-    sums_out,
     sums_in,
     in_sem,
     weight_sem,
@@ -68,7 +67,7 @@
     modes = decay_ref.shape[0]
     groups = channels // LANES
     seg = rows // SEGS
-    tile = min(256, channels)
+    tile = min(512, channels)
     tiles = channels // tile
 
     def in_copy(d, j):
@@ -109,6 +108,14 @@
         one_hot, embed_ref[...], (((0,), (0,)), ((), ())), preferred_element_type=jnp.float32
     )
     gathered[shard] = stream.astype(jnp.bfloat16)
+    ones = jnp.ones((8, channels), jnp.float32)
+    squares_out[...] = lax.dot_general(
+        ones,
+        stream * stream,
+        (((1,), (1,)), ((), ())),
+        precision=lax.Precision.HIGHEST,
+        preferred_element_type=jnp.float32,
+    )
     pl.semaphore_wait(barrier, seq_size - 1 + chan_size - 1)
 
     def square_copy(to, source):
@@ -141,18 +148,10 @@
         def _():
             gather_copy(1, which, shard - 1).start()
 
+    for k in range(1, chan_size):
+        square_copy(lax.rem(shard + k, chan_size), shard).start()
     send_up(shard)
     send_down(shard)
-    ones = jnp.ones((8, channels), jnp.float32)
-    squares_out[...] = lax.dot_general(
-        ones,
-        stream * stream,
-        (((1,), (1,)), ((), ())),
-        precision=lax.Precision.HIGHEST,
-        preferred_element_type=jnp.float32,
-    )
-    for k in range(1, chan_size):
-        square_copy(lax.rem(shard + k, chan_size), shard).start()
     proj[...] = jnp.zeros_like(proj)
     total = squares_out[...]
     for k in range(1, chan_size):
@@ -360,7 +359,7 @@
 
     def sum_copy(way, dest, to):
         return pltpu.make_async_remote_copy(
-            src_ref=sums_out.at[way, dest],
+            src_ref=in_buf.at[dest, way, pl.ds(0, rows), :],
             dst_ref=sums_in.at[way, dest],
             send_sem=sum_send_sem.at[way, dest],
             recv_sem=sum_recv_sem.at[way, dest],
@@ -374,13 +373,13 @@
         @pl.when(has_earlier)
         def _():
             sum_copy(way, dest, to).wait_recv()
-            sums_out[way, dest] = (part[...] + sums_in[way, dest].astype(jnp.float32)).astype(
+            in_buf[dest, way, :rows, :] = (part[...] + sums_in[way, dest].astype(jnp.float32)).astype(
                 jnp.bfloat16
             )
 
         @pl.when(jnp.logical_not(has_earlier))
         def _():
-            sums_out[way, dest] = part[...].astype(jnp.bfloat16)
+            in_buf[dest, way, :rows, :] = part[...].astype(jnp.bfloat16)
 
         sum_copy(way, dest, to).start()
 
@@ -486,7 +485,6 @@
             pltpu.VMEM((rows, channels), bf16),
             pltpu.VMEM((rows, channels), f32),
             pltpu.VMEM((2, chan_size, rows, channels), bf16),
-            pltpu.VMEM((2, chan_size, rows, channels), bf16),
             dma((chan_size, FEAT)),
             dma((chan_size,)),
             dma((chan_size,)),
@@ -500,7 +498,7 @@
             dma((2, chan_size)),
         ],
         compiler_params=pltpu.CompilerParams(
-            collective_id=0, has_side_effects=True, vmem_limit_bytes=60 << 20
+            collective_id=0, has_side_effects=True, vmem_limit_bytes=54 << 20
         ),
     )(
         tokens.reshape(1, rows),

time: 110 us -> 104 us (0.945)
  Pallas kernels: 108 us -> 102 us
    pallas_call x1, Pallas kernels: 108 us -> 102 us  [on_device(): pl.pallas_call(functools.partial(block_kernel, seq_size, chan_size), out_...]
where the time goes in v6:
time: 104 us
  Pallas kernels  102 us (98%)
  local copies, waits for them, and re-layouts  1.87 us (2%)
    pallas_call x1, Pallas kernels, on_device(): pl.pallas_call(functools.partial(block_kernel, seq_size, chan_size), out_...  102 us

profile of v6, /device:TPU:0, one launch (start us, length us, event | category | flops | bytes accessed | tf_op | source)
XLA Modules:
  0.0 103.5 jit_solution(11454223811206386065)
XLA Ops:
  0.0 101.7 %shard_map.91 = bf16[256,1024]{1,0:T(8,128)(2,1)} custom-call(s32[1,256]{1,0:T(1,128)} %bitcast.7, bf16[512,1024]{1,0:T(8,128)(2,1)} %embed_ref.1, f32[1,4096]{1,0:T(1,128)} %bitcast.5, f32[3,3,1024]{2,1,0:T(4,128)} %filter_ref.1, f32[16,1024]{1,0:T(8,128)} %decay_ref.1, f32[16,1024]{1,0:T(8,128)} %residue_ref.1, f32[1,1024]{1,0:T(1,128)} %bitcast.6, ...), custom_call_target="tpu_custom_call" | custom-call | tf_op jit(solution)/shard_map/pallas_call | solution.py:461
  101.7 1.9 %copy.11 = bf16[256,1024]{1,0:T(8,128)(2,1)} copy(bf16[256,1024]{1,0:T(8,128)(2,1)} %shard_map.91) | data formatting | bytes 1048576
